TPU v7x, 128 devices: a whole 4x4x4 slice. The times are simulated.
128 devices in a mesh: gz: 32 (over x, z, y_lo), gy: 2 (over core), gx: 2 (over y_hi).
Axes of the slice: x: 4, y: 4 (y_hi: 2, y_lo: 2; y = y_hi * 2 + y_lo), z: 4, core: 2. Of those that a mesh axis runs over, the one named last changes fastest.
Arguments:
- positions: float32 [8192, 3, 128], P(('gz', 'gy', 'gx')), may hold values from 0 to 4
- velocities: float32 [8192, 3, 128], P(('gz', 'gy', 'gx')), may hold values from -6 to 6
- charges: float32 [8192, 128], P(('gz', 'gy', 'gx')), may hold values from -4 to 4
- atom_types: int32 [8192, 128], P(('gz', 'gy', 'gx')), may hold values from 0 to 15
- type_radius: float32 [16], replicated, may hold values from 0.3 to 1
- tiles: int32 [32768, 2], P(('gz', 'gy', 'gx')), may hold values from 0 to 383
- tile_live: int32 [128], P(('gz', 'gy', 'gx')), may hold values from 32 to 256, as said below
- destinations: int32 [8192, 1], P(('gz', 'gy', 'gx')), may hold values from 0 to 31; in each aligned block of 64 rows (0 to 63, 64 to 127, ...) at most 4 rows name the same one
Outputs:
- forces: float32 [8192, 3, 128], P(('gz', 'gy', 'gx'))
- arrived: float32 [16384, 8, 128], P(('gz', 'gy', 'gx'))
Inputs may be any that keep to these rules, and one draw needn't show every extreme that they name: Each device's used tiles are the first tile_live entries of its list; some device uses all 256. `destinations`: among the rows of one device, at most 4 name the same destination; some destination gets exactly 4 from some device.
All inputs are finite; a program needn't handle non-finite values.
Results may differ from a plain program's by a relative error of at most 0.0003.
Values sent between devices are 32-bit elements; how exact they have to be, the bound alone decides.
A program may use at most 64 MiB of HBM per device.

v0:
```python
import jax
import jax.numpy as jnp
from jax import lax
from jax.sharding import PartitionSpec as P

STEPS = 2


coulomb = 0.3
time_step = 0.05
tile_group = 8


def whole_of(array, axes, dim):
    for axis in reversed(axes):
        array = lax.all_gather(array, axis, axis=dim, tiled=True)
    return array


def extended(cells, sides, width):
    for axis, dim in sides:
        count = lax.axis_size(axis)
        head = lax.slice_in_dim(cells, 0, width, axis=dim)
        tail = lax.slice_in_dim(cells, cells.shape[dim] - width, cells.shape[dim], axis=dim)
        cells = jnp.concatenate(
            [
                lax.ppermute(tail, axis, [(i, (i + 1) % count) for i in range(count)]),
                cells,
                lax.ppermute(head, axis, [((i + 1) % count, i) for i in range(count)]),
            ],
            axis=dim,
        )
    return cells


def cut_along(array, dim, size):
    before, after = (array.shape[:dim], array.shape[dim + 1 :])
    return jnp.moveaxis(array.reshape(*before, size, -1, *after), dim, 0)


def summed_on_arrival(array, axis, dim):
    size = lax.axis_size(axis)
    pieces = lax.all_to_all(cut_along(array, dim, size), axis, 0, 0, tiled=True)
    return jnp.sum(pieces, axis=0)


def passed_along(value, axis, steps):
    count = lax.axis_size(axis)
    pairs = [(source, (source + steps) % count) for source in range(count)]
    return lax.ppermute(value, axis, pairs)


def tile_forces(packed, tile_pairs, live_count):

    def one_group(group_index, totals):
        first_tile = group_index * tile_group
        chosen = lax.dynamic_slice_in_dim(tile_pairs, first_tile, tile_group, 0)
        left_ids = chosen[:, 0]
        right_ids = chosen[:, 1]
        active = (first_tile + jnp.arange(tile_group, dtype=jnp.int32) < live_count).astype(
            jnp.float32
        )
        left_atoms = packed[left_ids]
        right_atoms = packed[right_ids]
        offset = left_atoms[:, 0:3, :, None] - right_atoms[:, 0:3, None, :]
        dist_sq = jnp.sum(offset * offset, axis=1)
        soften = left_atoms[:, 4, :, None] + right_atoms[:, 4, None, :]
        denominator = dist_sq + soften * soften
        strength = (
            coulomb
            * left_atoms[:, 3, :, None]
            * right_atoms[:, 3, None, :]
            / (denominator * jnp.sqrt(denominator))
        )
        strength = strength * active[:, None, None]
        pushed = strength[:, None] * offset
        on_left = jnp.sum(pushed, axis=3)
        on_right = -jnp.sum(pushed, axis=2)
        return totals.at[left_ids].add(on_left).at[right_ids].add(on_right)

    zeros = jnp.zeros((packed.shape[0], 3, packed.shape[2]), jnp.float32)
    last_group = (live_count + tile_group - 1) // tile_group
    return lax.fori_loop(0, last_group, one_group, zeros)


def local(positions, velocities, charges, atom_types, type_radius, tiles, tile_live, destinations):
    clusters = positions.shape[0]
    width = positions.shape[2]
    type_ids = jnp.arange(type_radius.shape[0], dtype=jnp.int32)
    atom_radii = jnp.sum(jnp.where(atom_types[..., None] == type_ids, type_radius, 0.0), axis=-1)
    live_count = tile_live[0]
    places = positions
    moving = velocities
    forces = jnp.zeros_like(positions)
    for step_index in range(STEPS):
        packed = jnp.concatenate([places, charges[:, None], atom_radii[:, None]], axis=1)
        plate_rows = whole_of(packed, ("gy", "gx"), 0)
        tower_rows = extended(packed, (("gz", 0),), clusters)
        buffer = jnp.concatenate(
            [plate_rows, tower_rows[:clusters], tower_rows[2 * clusters :]], axis=0
        )
        partial_value = tile_forces(buffer, tiles, live_count)
        plate_size = plate_rows.shape[0]
        home_forces = summed_on_arrival(partial_value[:plate_size], ("gy", "gx"), 0)
        returning = (
            (-1, partial_value[plate_size : plate_size + clusters]),
            (1, partial_value[plate_size + clusters :]),
        )
        for towards, portion in returning:
            home_forces = home_forces + passed_along(portion, "gz", towards)
        forces = home_forces
        moving = moving + time_step * forces
        places = places + time_step * moving
    carried = jnp.concatenate([places, moving, charges[:, None], atom_radii[:, None]], axis=1)
    groups = lax.axis_size("gz")
    capacity = max(2, 2 * clusters // groups)
    slot_count = groups * capacity
    target_ids = destinations[:, 0]
    onehot = (target_ids[:, None] == jnp.arange(groups, dtype=jnp.int32)[None, :]).astype(jnp.int32)
    rank_before = jnp.cumsum(onehot, axis=0) - onehot
    position = jnp.sum(rank_before * onehot, axis=1) + target_ids * capacity
    select = (position[None, :] == jnp.arange(slot_count, dtype=jnp.int32)[:, None]).astype(
        jnp.float32
    )
    sent_slots = jnp.einsum("sc,cfa->sfa", select, carried, precision=lax.Precision.HIGHEST)
    received = lax.all_to_all(
        sent_slots.reshape(groups, capacity, 8, width),
        "gz",
        split_axis=0,
        concat_axis=0,
        tiled=True,
    )
    return (forces, received.reshape(slot_count, 8, width))


def solution(mesh):
    placed = (
        P(("gz", "gy", "gx"), None, None),
        P(("gz", "gy", "gx"), None, None),
        P(("gz", "gy", "gx"), None),
        P(("gz", "gy", "gx"), None),
        P(),
        P(("gz", "gy", "gx"), None),
        P(("gz", "gy", "gx")),
        P(("gz", "gy", "gx"), None),
    )
    return jax.shard_map(
        local,
        mesh=mesh,
        in_specs=placed,
        out_specs=(P(("gz", "gy", "gx"), None, None), P(("gz", "gy", "gx"), None, None)),
        check_vma=False,
    )
```

profile of v0, /device:TPU:0, one launch (start us, length us, event | category | flops | bytes accessed | tf_op | source)
XLA Modules:
  0.0 441.6 jit_solution(3155410354105782110)
XLA Ops:
  0.6 1.0 select_reduce_fusion
  2.6 1.7 collective-permute-start
  4.3 5.8 %collective-permute-start.1 = (f32[64,5,128]{2,0,1:T(8,128)S(1)}, f32[64,5,128]{2,0,1:T(8,128)S(1)}, u32[]{:S(2)}, u32[]{:S(2)}) collective-permute-start(f32[64,5,128]{2,0,1:T(8,128)S(1)} %pad_maximum_fusion.3), channel_id=1, source_target_pairs={{4,0},{8,4},{12,8},{16,12},{20,16},{24,20},{28,24},{32,28},{36,32}... | collective-permute-start | bytes 491528 | tf_op jit(solution)/shard_map/ppermute | solution.py:29
  10.7 8.4 %all_gather.12 = f32[128,5,128]{2,0,1:T(8,128)S(1)} all-gather(f32[64,5,128]{2,0,1:T(8,128)S(1)} %pad_maximum_fusion.3), channel_id=1, replica_groups=mesh['gz'=32,'gy'=2,'gx'=2] {'gx'}, dimensions={0}, use_global_device_ids=true | all-gather | bytes 491520 | tf_op jit(solution)/shard_map/all_gather | solution.py:16
  19.9 2.3 all_gather.13
  23.0 124.1 %while.20 = (s32[]{:T(128)}, f32[384,3,128]{2,1,0:T(4,128)S(1)}, s32[]{:T(128)}, s32[256,2]{0,1:T(2,128)S(1)}, f32[384,5,128]{2,1,0:T(8,128)S(1)}, /*index=5*/s3...) while((s32[]{:T(128)}, f32[384,3,128]{2,1,0:T(4,128)S(1)}, s32[]{:T(128)}, s32[256,2]{0,1:T(2,128)S(1)}, ...), condition=%wide.region_7.8_spmd, body=%wide.region_1.7_spmd.sunk | while | flops 3545166 | bytes 2458271 | solution.py:83
  25.8 1.0 fusion.45
  31.2 1.0 fusion.45
  36.6 1.0 fusion.45
  42.0 1.0 fusion.45
  47.4 1.0 fusion.45
  52.8 1.0 fusion.45
  58.2 1.0 fusion.45
  63.6 1.0 fusion.45
  69.0 1.0 fusion.45
  74.4 1.0 fusion.45
  79.8 1.0 fusion.45
  85.2 1.0 fusion.45
  90.6 1.0 fusion.45
  96.0 1.0 fusion.45
  101.4 1.0 fusion.45
  106.8 1.0 fusion.45
  112.2 1.0 fusion.45
  117.6 1.0 fusion.45
  123.0 1.0 fusion.45
  128.4 1.0 fusion.45
  133.8 1.0 fusion.45
  139.2 1.0 fusion.45
  144.5 1.0 fusion.45
  148.1 25.0 %all-to-all-start = ((f32[4,64,3,128]{3,1,2,0:T(8,128)}), f32[4,64,3,128]{3,1,2,0:T(8,128)S(1)}, u32[]{:S(2)}, u32[]{:S(2)}) async-start(f32[4,64,3,128]{3,1,2,0:T(8,128)} %copy.48), calls=%async_computation | async-start | bytes 786432 | tf_op jit(solution)/shard_map/all_to_all | solution.py:43
  173.0 31.8 %collective-permute-start.2 = (f32[64,3,128]{2,0,1:T(8,128)S(1)}, f32[64,3,128]{2,0,1:T(8,128)S(1)}, u32[]{:S(2)}, u32[]{:S(2)}) collective-permute-start(f32[64,3,128]{2,0,1:T(8,128)S(1)} %get-tuple-element.163), channel_id=1, source_target_pairs={{0,124},{4,0},{8,4},{12,8},{16,12},{20,16},{24,20},{28,24},{32,28}... | collective-permute-start | bytes 294920 | tf_op jit(solution)/shard_map/ppermute | solution.py:50
  205.1 2.5 collective-permute-done.2
  207.5 6.4 %collective-permute-done.3 = f32[64,3,128]{2,0,1:T(8,128)S(1)} collective-permute-done((f32[64,3,128]{2,0,1:T(8,128)S(1)}, f32[64,3,128]{2,0,1:T(8,128)S(1)}, u32[]{:S(2)}, u32[]{:S(2)}) %collective-permute-start.3) | collective-permute-done | bytes 98336 | tf_op jit(solution)/shard_map/ppermute | solution.py:50
  214.0 7.8 %all_gather.14 = f32[128,5,128]{2,0,1:T(8,128)S(1)} all-gather(f32[64,5,128]{2,0,1:T(8,128)S(1)} %pad_maximum_fusion.2), channel_id=1, replica_groups=mesh['gz'=32,'gy'=2,'gx'=2] {'gx'}, dimensions={0}, use_global_device_ids=true | all-gather | bytes 491520 | tf_op jit(solution)/shard_map/all_gather | solution.py:16
  221.9 6.2 %collective-permute-start.5 = (f32[64,5,128]{2,0,1:T(8,128)S(1)}, f32[64,5,128]{2,0,1:T(8,128)S(1)}, u32[]{:S(2)}, u32[]{:S(2)}) collective-permute-start(f32[64,5,128]{2,0,1:T(8,128)S(1)} %pad_maximum_fusion.2), channel_id=1, source_target_pairs={{4,0},{8,4},{12,8},{16,12},{20,16},{24,20},{28,24},{32,28},{36,32}... | collective-permute-start | bytes 491528 | tf_op jit(solution)/shard_map/ppermute | solution.py:29
  228.1 2.3 all_gather.15
  230.4 1.0 collective-permute-done.4
  232.2 124.1 %while.21 = (s32[]{:T(128)}, f32[384,3,128]{2,1,0:T(4,128)S(1)}, s32[]{:T(128)}, s32[256,2]{0,1:T(2,128)S(1)}, f32[384,5,128]{2,1,0:T(8,128)S(1)}, /*index=5*/s3...) while((s32[]{:T(128)}, f32[384,3,128]{2,1,0:T(4,128)S(1)}, s32[]{:T(128)}, s32[256,2]{0,1:T(2,128)S(1)}, ...), condition=%wide.region_15.16_spmd, body=%wide.region_9.15_spmd.sunk | while | flops 3545166 | bytes 2458271 | solution.py:83
  235.0 1.0 fusion.50
  240.4 1.0 fusion.50
  245.8 1.0 fusion.50
  262.0 1.0 fusion.50
  332.1 1.0 fusion.50
  357.2 25.6 %all-to-all-start.1 = ((f32[4,64,3,128]{3,1,2,0:T(8,128)}), f32[4,64,3,128]{3,1,2,0:T(8,128)S(1)}, u32[]{:S(2)}, u32[]{:S(2)}) async-start(f32[4,64,3,128]{3,1,2,0:T(8,128)} %copy.55), calls=%async_computation.1 | async-start | bytes 786432 | tf_op jit(solution)/shard_map/all_to_all | solution.py:43
  382.8 32.8 %collective-permute-start.6 = (f32[64,3,128]{2,0,1:T(8,128)S(1)}, f32[64,3,128]{2,0,1:T(8,128)S(1)}, u32[]{:S(2)}, u32[]{:S(2)}) collective-permute-start(f32[64,3,128]{2,0,1:T(8,128)S(1)} %get-tuple-element.161), channel_id=1, source_target_pairs={{0,124},{4,0},{8,4},{12,8},{16,12},{20,16},{24,20},{28,24},{32,28}... | collective-permute-start | bytes 294920 | tf_op jit(solution)/shard_map/ppermute | solution.py:50
  415.6 2.6 collective-permute-done.6
  418.2 6.4 %collective-permute-done.7 = f32[64,3,128]{2,0,1:T(8,128)S(1)} collective-permute-done((f32[64,3,128]{2,0,1:T(8,128)S(1)}, f32[64,3,128]{2,0,1:T(8,128)S(1)}, u32[]{:S(2)}, u32[]{:S(2)}) %collective-permute-start.7) | collective-permute-done | bytes 98336 | tf_op jit(solution)/shard_map/ppermute | solution.py:50
  426.0 14.8 %all_to_all.15 = f32[32,4,8,128]{3,1,2,0:T(4,128)S(1)} all-to-all(f32[32,4,8,128]{3,1,2,0:T(4,128)S(1)} %copy.60), channel_id=1, replica_groups=mesh['gz'=32,'gy'=2,'gx'=2] {'gz'}, dimensions={0} | all-to-all | bytes 1048576 | tf_op jit(solution)/shard_map/all_to_all | solution.py:126
  (753 shorter events, 222.3 us)
Async XLA Ops:
  2.6 19.6 %collective-permute-start = (f32[64,5,128]{2,0,1:T(8,128)S(1)}, f32[64,5,128]{2,0,1:T(8,128)S(1)}, u32[]{:S(2)}, u32[]{:S(2)}) collective-permute-start(f32[64,5,128]{2,0,1:T(8,128)S(1)} %pad_maximum_fusion.3), channel_id=1, source_target_pairs={{0,4},{4,8},{8,12},{12,16},{16,20},{20,24},{24,28},{28,32},{32,36}... | collective-permute-start | bytes 491528 | tf_op jit(solution)/shard_map/ppermute | solution.py:27
  4.3 17.9 %collective-permute-start.1 = (f32[64,5,128]{2,0,1:T(8,128)S(1)}, f32[64,5,128]{2,0,1:T(8,128)S(1)}, u32[]{:S(2)}, u32[]{:S(2)}) collective-permute-start(f32[64,5,128]{2,0,1:T(8,128)S(1)} %pad_maximum_fusion.3), channel_id=1, source_target_pairs={{4,0},{8,4},{12,8},{16,12},{20,16},{24,20},{28,24},{32,28},{36,32}... | collective-permute-start | bytes 491528 | tf_op jit(solution)/shard_map/ppermute | solution.py:29
  22.3 0.7 copy-start.3
  147.2 57.7 %copy-start.4 = (s32[64,1]{0,1:T(1,128)S(1)}, s32[64,1]{0,1:T(1,128)}, u32[]{:S(2)}) copy-start(s32[64,1]{0,1:T(1,128)} %param.19) | copy-start | bytes 772
  147.2 66.8 %copy-start = (f32[64,3,128]{2,0,1:T(8,128)S(1)}, f32[64,3,128]{2,0,1:T(8,128)}, u32[]{:S(2)}) copy-start(f32[64,3,128]{2,0,1:T(8,128)} %param.12) | copy-start | bytes 294916
  147.2 66.7 %copy-start.2 = (f32[64,3,128]{2,0,1:T(8,128)S(1)}, f32[64,3,128]{2,0,1:T(8,128)}, u32[]{:S(2)}) copy-start(f32[64,3,128]{2,0,1:T(8,128)} %param.13) | copy-start | bytes 294916
  147.3 66.7 %copy-start.1 = (f32[64,128]{1,0:T(8,128)S(1)}, f32[64,128]{1,0:T(8,128)}, u32[]{:S(2)}) copy-start(f32[64,128]{1,0:T(8,128)} %param.14) | copy-start | bytes 98308
  148.1 57.0 %all-to-all-start = ((f32[4,64,3,128]{3,1,2,0:T(8,128)}), f32[4,64,3,128]{3,1,2,0:T(8,128)S(1)}, u32[]{:S(2)}, u32[]{:S(2)}) async-start(f32[4,64,3,128]{3,1,2,0:T(8,128)} %copy.48), calls=%async_computation | async-start | bytes 786432 | tf_op jit(solution)/shard_map/all_to_all | solution.py:43
  173.0 34.5 %collective-permute-start.2 = (f32[64,3,128]{2,0,1:T(8,128)S(1)}, f32[64,3,128]{2,0,1:T(8,128)S(1)}, u32[]{:S(2)}, u32[]{:S(2)}) collective-permute-start(f32[64,3,128]{2,0,1:T(8,128)S(1)} %get-tuple-element.163), channel_id=1, source_target_pairs={{0,124},{4,0},{8,4},{12,8},{16,12},{20,16},{24,20},{28,24},{32,28}... | collective-permute-start | bytes 294920 | tf_op jit(solution)/shard_map/ppermute | solution.py:50
  204.9 9.1 %collective-permute-start.3 = (f32[64,3,128]{2,0,1:T(8,128)S(1)}, f32[64,3,128]{2,0,1:T(8,128)S(1)}, u32[]{:S(2)}, u32[]{:S(2)}) collective-permute-start(f32[64,3,128]{2,0,1:T(8,128)S(1)} %get-tuple-element.164), channel_id=1, source_target_pairs={{0,4},{4,8},{8,12},{12,16},{16,20},{20,24},{24,28},{28,32},{32,36}... | collective-permute-start | bytes 294920 | tf_op jit(solution)/shard_map/ppermute | solution.py:50
  221.8 9.5 %collective-permute-start.4 = (f32[64,5,128]{2,0,1:T(8,128)S(1)}, f32[64,5,128]{2,0,1:T(8,128)S(1)}, u32[]{:S(2)}, u32[]{:S(2)}) collective-permute-start(f32[64,5,128]{2,0,1:T(8,128)S(1)} %pad_maximum_fusion.2), channel_id=1, source_target_pairs={{0,4},{4,8},{8,12},{12,16},{16,20},{20,24},{24,28},{28,32},{32,36}... | collective-permute-start | bytes 491528 | tf_op jit(solution)/shard_map/ppermute | solution.py:27
  221.9 9.5 %collective-permute-start.5 = (f32[64,5,128]{2,0,1:T(8,128)S(1)}, f32[64,5,128]{2,0,1:T(8,128)S(1)}, u32[]{:S(2)}, u32[]{:S(2)}) collective-permute-start(f32[64,5,128]{2,0,1:T(8,128)S(1)} %pad_maximum_fusion.2), channel_id=1, source_target_pairs={{4,0},{8,4},{12,8},{16,12},{20,16},{24,20},{28,24},{32,28},{36,32}... | collective-permute-start | bytes 491528 | tf_op jit(solution)/shard_map/ppermute | solution.py:29
  357.2 58.4 %all-to-all-start.1 = ((f32[4,64,3,128]{3,1,2,0:T(8,128)}), f32[4,64,3,128]{3,1,2,0:T(8,128)S(1)}, u32[]{:S(2)}, u32[]{:S(2)}) async-start(f32[4,64,3,128]{3,1,2,0:T(8,128)} %copy.55), calls=%async_computation.1 | async-start | bytes 786432 | tf_op jit(solution)/shard_map/all_to_all | solution.py:43
  382.8 35.5 %collective-permute-start.6 = (f32[64,3,128]{2,0,1:T(8,128)S(1)}, f32[64,3,128]{2,0,1:T(8,128)S(1)}, u32[]{:S(2)}, u32[]{:S(2)}) collective-permute-start(f32[64,3,128]{2,0,1:T(8,128)S(1)} %get-tuple-element.161), channel_id=1, source_target_pairs={{0,124},{4,0},{8,4},{12,8},{16,12},{20,16},{24,20},{28,24},{32,28}... | collective-permute-start | bytes 294920 | tf_op jit(solution)/shard_map/ppermute | solution.py:50
  415.6 9.1 %collective-permute-start.7 = (f32[64,3,128]{2,0,1:T(8,128)S(1)}, f32[64,3,128]{2,0,1:T(8,128)S(1)}, u32[]{:S(2)}, u32[]{:S(2)}) collective-permute-start(f32[64,3,128]{2,0,1:T(8,128)S(1)} %get-tuple-element.162), channel_id=1, source_target_pairs={{0,4},{4,8},{8,12},{12,16},{16,20},{20,24},{24,28},{28,32},{32,36}... | collective-permute-start | bytes 294920 | tf_op jit(solution)/shard_map/ppermute | solution.py:50
where the time goes:
time: 443 us; the launch traced here: 442 us
  other arithmetic  191 us (43%)
  starting transfers between devices  129 us (29%)
  local copies, waits for them, and re-layouts  59.5 us (13%)
  blocking collectives  35.6 us (8%)
  waiting for transfers between devices  19 us (4%)
  loops' own time  5.43 us (1%)
    scatter-add x92, other arithmetic, one_group(): return totals.at[left_ids].add(on_left).at[right_ids].add(on_right)  71.7 us
    ppermute x4, starting transfers between devices, passed_along(): return lax.ppermute(value, axis, pairs)  64.6 us
    all_to_all x2, starting transfers between devices, summed_on_arrival(): pieces = lax.all_to_all(cut_along(array, dim, size), axis, 0, 0, tiled=True)  50.5 us
    reduce_sum x46, other arithmetic, one_group(): on_right = -jnp.sum(pushed, axis=2)  45.9 us
    convert_element_type x46, other arithmetic, one_group(): (first_tile + jnp.arange(tile_group, dtype=jnp.int32) < live_count).astyp...  29.9 us
    gather x46, local copies, waits for them, and re-layouts, one_group(): left_atoms = packed[left_ids]  25.5 us
    gather x46, local copies, waits for them, and re-layouts, one_group(): right_atoms = packed[right_ids]  25.4 us
    reduce_sum x46, other arithmetic, one_group(): dist_sq = jnp.sum(offset * offset, axis=1)  21.7 us
  transfers between devices with their start and end apart: 10, of which 5 were waited for; matrix products, arithmetic and copies ran while one was open for 0% of the time, Pallas kernels for 0%

commit v1 on v0

v1 whole, which is shorter than its diff:
```python
import functools

import jax
import jax.numpy as jnp
from jax import lax
from jax.experimental import pallas as pl
from jax.experimental.pallas import tpu as pltpu
from jax.sharding import PartitionSpec as P

coulomb = 0.3
time_step = 0.05

MESH = pl.DeviceIdType.MESH
F32 = jnp.float32
BF16 = jnp.bfloat16

CL = 64
LANES = 128
SLOTS = 6
ROWS = SLOTS * CL
CAPACITY = 4
TOWERS = 32
ARRIVING = TOWERS * CAPACITY
UNROLL = 16
CENTER = 2.0
PLANES = 39
ENDS = 20
CHARGED = 31


def split(x):
    high = x.astype(BF16).astype(F32)
    rest = x - high
    middle = rest.astype(BF16).astype(F32)
    return high, middle, rest - middle


def tile_kernel(tiles, live, places, fixed, out, planes, totals):
    def prepare(group, carry):
        slot, inner = group // (CL // 8), group % (CL // 8)
        rows = pl.ds(pl.multiple_of(inner * 8, 8), 8)
        to = pl.multiple_of(group * 8, 8)

        def put(plane, value):
            planes[pl.ds(plane * ROWS + to, 8), :] = value

        x = [places[slot, c, rows, :] - CENTER for c in range(3)]
        q = fixed[slot, 3, rows, :]
        radius = fixed[slot, 4, rows, :]
        half = 0.5 * (x[0] * x[0] + x[1] * x[1] + x[2] * x[2] + radius * radius)
        for c, value in enumerate(x + [radius]):
            high, middle, low = split(value)
            put(c, high)
            put(4 + c, middle)
            put(8 + c, high)
            put(12 + c, low)
            put(16 + c, high)
        parts = split(half)
        one = jnp.ones_like(half)
        for c in range(3):
            put(ENDS + c, one)
            put(ENDS + 3 + c, parts[c])
            put(ENDS + 6 + c, one)
        zero = jnp.zeros_like(half)
        put(ENDS + 9, zero)
        put(ENDS + 10, zero)
        for c, value in enumerate([q * x[0], q * x[1], q * x[2], q]):
            high = value.astype(BF16).astype(F32)
            put(CHARGED + c, high)
            put(CHARGED + 4 + c, value - high)
        for k in range(8):
            totals[pl.ds(pl.multiple_of(group * 64, 64) + k * 8, 8), :] = zero
        return carry

    lax.fori_loop(0, ROWS // 8, prepare, 0)

    sign = jnp.where(lax.broadcasted_iota(jnp.int32, (8, LANES), 0) % 4 == 3, 1.0, -1.0).astype(F32)
    live_count = live[0]

    def eight(plane, row):
        return planes[pl.ds(plane * ROWS + row, 8, stride=ROWS), :]

    def one_group(group, carry):
        sums = []
        ids = [(tiles[0, group * UNROLL + u], tiles[1, group * UNROLL + u]) for u in range(UNROLL)]
        blank = jnp.zeros((32, LANES), F32)
        halves = []
        for u in range(0, UNROLL, 2):
            lefts, rights = [], []
            for a, b in ids[u : u + 2]:
                near = eight(0, a) * sign
                lefts += [near, near, eight(12, a) * sign, eight(ENDS + 3, a)]
                rights.append(jnp.concatenate([eight(0, b), eight(4, b), eight(8, b), eight(ENDS, b)], axis=0))
            left = jnp.concatenate(lefts, axis=0)
            right = jnp.concatenate(
                [
                    jnp.concatenate([rights[0], blank], axis=1),
                    jnp.concatenate([blank, rights[1]], axis=1),
                ],
                axis=0,
            )
            halves.append(
                lax.dot_general(
                    left.astype(BF16), right.astype(BF16), (((0,), (0,)), ((), ())), preferred_element_type=F32
                )
            )
        powers = []
        for half_dist in halves:
            root = lax.rsqrt(half_dist)
            power = root * root * root
            high = power.astype(BF16)
            powers.append((high, (power - high.astype(F32)).astype(BF16)))
        for u in range(0, UNROLL, 2):
            high, low = powers[u // 2]
            active = [
                jnp.where(group * UNROLL + u + v < live_count, 1.0, 0.0).astype(F32) for v in range(2)
            ]
            from_a = jnp.concatenate([eight(CHARGED, ids[u + v][0]) * active[v] for v in range(2)], axis=0).astype(BF16)
            from_b = jnp.concatenate([eight(CHARGED, ids[u + v][1]) * active[v] for v in range(2)], axis=0).astype(BF16)
            on_right = jnp.dot(
                jnp.concatenate([from_a, from_a], axis=1), jnp.concatenate([high, low], axis=0), preferred_element_type=F32
            )
            across = jnp.concatenate(
                [
                    jnp.concatenate([high[:, :LANES], low[:, :LANES]], axis=1),
                    jnp.concatenate([high[:, LANES:], low[:, LANES:]], axis=1),
                ],
                axis=0,
            )
            on_left = lax.dot_general(
                jnp.concatenate([from_b, from_b], axis=1), across, (((1,), (1,)), ((), ())), preferred_element_type=F32
            )
            sums.append((ids[u][0], on_left[0:8, :LANES]))
            sums.append((ids[u][1], on_right[0:8, :LANES]))
            sums.append((ids[u + 1][0], on_left[8:16, LANES:]))
            sums.append((ids[u + 1][1], on_right[8:16, LANES:]))
        for row, value in sums:
            at = pl.ds(pl.multiple_of(row * 8, 8), 8)
            totals[at, :] = totals[at, :] + value
        return carry

    lax.fori_loop(0, (live_count + UNROLL - 1) // UNROLL, one_group, 0)

    factor = coulomb * 0.5**1.5

    def finish(group, carry):
        slot, inner = group // (CL // 8), group % (CL // 8)
        rows = pl.ds(pl.multiple_of(inner * 8, 8), 8)

        def summed(channel):
            first = pl.multiple_of(group * 64, 64) + channel
            return totals[pl.ds(first, 8, stride=8), :] + totals[pl.ds(first + 4, 8, stride=8), :]

        scale = factor * fixed[slot, 3, rows, :]
        whole = summed(3)
        for c in range(3):
            out[slot, c, rows, :] = scale * ((places[slot, c, rows, :] - CENTER) * whole - summed(c))
        return carry

    lax.fori_loop(0, ROWS // 8, finish, 0)


def tile_forces(tiles, live, places, fixed):
    return pl.pallas_call(
        tile_kernel,
        out_shape=jax.ShapeDtypeStruct((SLOTS, 3, CL, LANES), F32),
        in_specs=[
            pl.BlockSpec(memory_space=pltpu.SMEM),
            pl.BlockSpec(memory_space=pltpu.SMEM),
            pl.BlockSpec(memory_space=pltpu.VMEM),
            pl.BlockSpec(memory_space=pltpu.VMEM),
        ],
        out_specs=pl.BlockSpec(memory_space=pltpu.VMEM),
        scratch_shapes=[
            pltpu.VMEM((PLANES * ROWS, LANES), F32),
            pltpu.VMEM((ROWS * 8, LANES), F32),
        ],
        compiler_params=pltpu.CompilerParams(vmem_limit_bytes=40 * 2**20),
        cost_estimate=pl.CostEstimate(flops=256 * 128 * 128 * 120, bytes_accessed=2 * 2**20, transcendentals=256 * 128 * 128),
    )(tiles, live, places, fixed)


VMEM = pl.BlockSpec(memory_space=pltpu.VMEM)
SMEM = pl.BlockSpec(memory_space=pltpu.SMEM)
BELOW, ABOVE = 4, 5


def here():
    return lax.axis_index("gz"), lax.axis_index("gy"), lax.axis_index("gx")


def neighbours():
    z, y, x = here()
    mine = y * 2 + x
    partners = []
    for dy, dx in ((0, 1), (1, 1), (1, 0)):
        oy, ox = (1 - y if dy else y), (1 - x if dx else x)
        partners.append(((z, oy, ox), oy * 2 + ox, mine))
    partners.append(((lax.rem(z + 1, TOWERS), y, x), ABOVE, BELOW))
    partners.append(((lax.rem(z + TOWERS - 1, TOWERS), y, x), BELOW, ABOVE))
    return mine, partners


def greet(devices):
    barrier = pltpu.get_barrier_semaphore()
    for device in devices:
        pl.semaphore_signal(barrier, inc=1, device_id=device, device_id_type=MESH)
    return barrier


def spread(buffer, send_sems, recv_sems):
    mine, partners = neighbours()
    copies = []
    for k, (device, there, back) in enumerate(partners):
        copy = pltpu.make_async_remote_copy(
            buffer.at[mine], buffer.at[back], send_sems.at[k], recv_sems.at[back], device_id=device, device_id_type=MESH
        )
        copy.start()
        copies.append(copy)
    for k, (device, there, back) in enumerate(partners):
        pltpu.make_async_remote_copy(
            buffer.at[there], buffer.at[there], send_sems.at[k], recv_sems.at[there], device_id=device, device_id_type=MESH
        ).wait_recv()
    for copy in copies:
        copy.wait_send()


def gather_forces(partial, landing, send_sems, recv_sems):
    mine, partners = neighbours()
    copies = []
    for k, (device, there, back) in enumerate(partners):
        copy = pltpu.make_async_remote_copy(
            partial.at[there], landing.at[back], send_sems.at[k], recv_sems.at[back], device_id=device, device_id_type=MESH
        )
        copy.start()
        copies.append(copy)
    total = [partial[mine, c] for c in range(3)]
    for k, (device, there, back) in enumerate(partners):
        pltpu.make_async_remote_copy(
            landing.at[there], landing.at[there], send_sems.at[k], recv_sems.at[there], device_id=device, device_id_type=MESH
        ).wait_recv()
        total = [total[c] + landing[there, c] for c in range(3)]
    for copy in copies:
        copy.wait_send()
    return total


def import_kernel(radii, positions, charges, types, buffer, send_sems, recv_sems):
    mine, partners = neighbours()
    barrier = greet([p[0] for p in partners])
    for c in range(3):
        buffer[mine, c] = positions[c]
    buffer[mine, 3] = charges[...]
    kinds = types[...]
    radius = jnp.zeros((CL, LANES), F32)
    for kind in range(16):
        radius = jnp.where(kinds == kind, radii[kind], radius)
    buffer[mine, 4] = radius
    pl.semaphore_wait(barrier, 5)
    spread(buffer, send_sems, recv_sems)


def step_kernel(partial, fixed, velocities, places, moving, landing, send_sems, recv_sems, next_send, next_recv):
    mine, partners = neighbours()
    barrier = greet([p[0] for p in partners])
    pl.semaphore_wait(barrier, 5)
    forces = gather_forces(partial, landing, send_sems, recv_sems)
    for c in range(3):
        speed = velocities[c] + time_step * forces[c]
        moving[c] = speed
        places[mine, c] = fixed[mine, c] + time_step * speed
    spread(places, next_send, next_recv)


def last_kernel(
    partial, fixed, places, moving, destinations, forces_out, arrived, landing, slots, send_sems, recv_sems, out_sems, in_sems, own_sem
):
    z, y, x = here()
    mine, partners = neighbours()
    others = [(lax.rem(z + k, TOWERS), y, x) for k in range(1, TOWERS)]
    barrier = greet([p[0] for p in partners[:3]] + others)

    row = jnp.broadcast_to(destinations[...].astype(F32), (CL, CL))
    r = lax.broadcasted_iota(jnp.int32, (CL, CL), 0)
    c = lax.broadcasted_iota(jnp.int32, (CL, CL), 1)
    column = jnp.sum(jnp.where(r == c, row, 0.0), axis=1, keepdims=True)
    rank = jnp.sum(jnp.where((column == row) & (r < c), 1.0, 0.0), axis=0, keepdims=True)
    slot = row[0:1] * CAPACITY + rank
    select = (lax.broadcasted_iota(jnp.int32, (ARRIVING, CL), 0).astype(F32) == slot).astype(BF16)

    pl.semaphore_wait(barrier, 3 + TOWERS - 1)
    forces = gather_forces(partial, landing, send_sems, recv_sems)
    carried = []
    speeds = []
    for k in range(3):
        forces_out[k] = forces[k]
        speed = moving[k] + time_step * forces[k]
        speeds.append(speed)
        carried.append(places[mine, k] + time_step * speed)
    carried = carried + speeds + [fixed[mine, 3], fixed[mine, 4]]
    for k, value in enumerate(carried):
        parts = split(value)
        slots[:, k, :] = sum(jnp.dot(select, part.astype(BF16), preferred_element_type=F32) for part in reversed(parts))

    def send(tower):
        return pltpu.make_async_remote_copy(
            slots.at[pl.ds(tower * CAPACITY, CAPACITY)],
            arrived.at[pl.ds(z * CAPACITY, CAPACITY)],
            out_sems.at[tower],
            in_sems.at[z],
            device_id=(tower, y, x),
            device_id_type=MESH,
        )

    def receive(tower):
        return pltpu.make_async_remote_copy(
            slots.at[pl.ds(tower * CAPACITY, CAPACITY)],
            arrived.at[pl.ds(tower * CAPACITY, CAPACITY)],
            out_sems.at[tower],
            in_sems.at[tower],
            device_id=(tower, y, x),
            device_id_type=MESH,
        )

    for k in range(1, TOWERS):
        send(lax.rem(z + k, TOWERS)).start()
    own = pltpu.make_async_copy(
        slots.at[pl.ds(z * CAPACITY, CAPACITY)], arrived.at[pl.ds(z * CAPACITY, CAPACITY)], own_sem
    )
    own.start()
    own.wait()
    for k in range(1, TOWERS):
        receive(lax.rem(z + TOWERS - k, TOWERS)).wait_recv()
    for k in range(1, TOWERS):
        send(lax.rem(z + k, TOWERS)).wait_send()


def params(number):
    return pltpu.CompilerParams(collective_id=number, has_side_effects=True, vmem_limit_bytes=40 * 2**20)


def dma(count):
    return pltpu.SemaphoreType.DMA((count,))


def local(positions, velocities, charges, atom_types, type_radius, tiles, tile_live, destinations):
    shape = functools.partial(jax.ShapeDtypeStruct, dtype=F32)
    pairs = tiles.T
    landing = pltpu.VMEM((SLOTS, 3, CL, LANES), F32)
    fixed = pl.pallas_call(
        import_kernel,
        out_shape=shape((SLOTS, 5, CL, LANES)),
        in_specs=[SMEM, VMEM, VMEM, VMEM],
        out_specs=VMEM,
        scratch_shapes=[dma(5), dma(6)],
        compiler_params=params(0),
    )(type_radius, jnp.swapaxes(positions, 0, 1), charges, atom_types)
    partial = tile_forces(pairs, tile_live, fixed, fixed)
    places, moving = pl.pallas_call(
        step_kernel,
        out_shape=(shape((SLOTS, 3, CL, LANES)), shape((3, CL, LANES))),
        in_specs=[VMEM] * 3,
        out_specs=(VMEM, VMEM),
        scratch_shapes=[landing, dma(5), dma(6), dma(5), dma(6)],
        compiler_params=params(1),
    )(partial, fixed, jnp.swapaxes(velocities, 0, 1))
    partial = tile_forces(pairs, tile_live, places, fixed)
    forces, arrived = pl.pallas_call(
        last_kernel,
        out_shape=(shape((3, CL, LANES)), shape((ARRIVING, 8, LANES))),
        in_specs=[VMEM] * 5,
        out_specs=(VMEM, VMEM),
        scratch_shapes=[
            landing,
            pltpu.VMEM((ARRIVING, 8, LANES), F32),
            dma(5),
            dma(6),
            dma(TOWERS),
            dma(TOWERS),
            pltpu.SemaphoreType.DMA,
        ],
        compiler_params=params(2),
    )(partial, fixed, places, moving, destinations.T)
    return jnp.swapaxes(forces, 0, 1), arrived


def solution(mesh):
    home = ("gz", "gy", "gx")
    placed = (
        P(home, None, None),
        P(home, None, None),
        P(home, None),
        P(home, None),
        P(),
        P(home, None),
        P(home),
        P(home, None),
    )
    return jax.shard_map(
        local,
        mesh=mesh,
        in_specs=placed,
        out_specs=(P(home, None, None), P(home, None, None)),
        check_vma=False,
    )
```

time: 443 us -> 113 us (0.26)
  other arithmetic: 191 us -> 0 us
  starting transfers between devices: 129 us -> 0 us
  Pallas kernels: 0 us -> 106 us
  local copies, waits for them, and re-layouts: 59.5 us -> 4.51 us
  blocking collectives: 35.6 us -> 0 us
  waiting for transfers between devices: 19 us -> 0 us
  loops' own time: 5.43 us -> 0 us
    pallas_call x0 -> x5, Pallas kernels: none -> 106 us  [the longest x2 38.2 us: tile_forces(): pl.pallas_call(tile_kernel, out_shape=jax.ShapeDtypeStruct((SLOTS, 3, CL,...]
    ppermute x8 -> x0, starting transfers between devices: 78.4 us -> none  [the longest x4 64.6 us: passed_along(): return lax.ppermute(value, axis, pairs)]
    scatter-add x92 -> x0, other arithmetic: 71.7 us -> none  [one_group(): return totals.at[left_ids].add(on_left).at[right_ids].add(on_right)]
    reduce_sum x96 -> x0, other arithmetic: 68.9 us -> none  [the longest x46 45.9 us: one_group(): on_right = -jnp.sum(pushed, axis=2)]
    gather x92 -> x0, local copies, waits for them, and re-layouts: 51 us -> none  [the longest x46 25.5 us: one_group(): left_atoms = packed[left_ids]]
    all_to_all x2 -> x0, starting transfers between devices: 50.5 us -> none  [summed_on_arrival(): pieces = lax.all_to_all(cut_along(array, dim, size), axis, 0, 0, tiled=True)]
    convert_element_type x47 -> x0, other arithmetic: 30.7 us -> none  [the longest x46 29.9 us: one_group(): (first_tile + jnp.arange(tile_group, dtype=jnp.int32) < live_count).astyp...]
    all_gather x4 -> x0, blocking collectives: 20.7 us -> none  [whole_of(): array = lax.all_gather(array, axis, axis=dim, tiled=True)]
  transfers between devices with their start and end apart: 10 -> 0, of which waited for: 5 -> 0; matrix products, arithmetic and copies ran while one was open for 0% -> 0% of each run, Pallas kernels for 0% -> 0%
where the time goes in v1:
time: 113 us; the launch traced here: 112 us
  Pallas kernels  106 us (94%)
  local copies, waits for them, and re-layouts  4.51 us (4%)
  between operations  1.37 us (1%)
    pallas_call x2, Pallas kernels, tile_forces(): pl.pallas_call(tile_kernel, out_shape=jax.ShapeDtypeStruct((SLOTS, 3, CL,...  38.2 us
    pallas_call x1, Pallas kernels, local(): pl.pallas_call(last_kernel, out_shape=(shape((3, CL, LANES)), shape((ARRI...  25.6 us
    pallas_call x1, Pallas kernels, local(): pl.pallas_call(step_kernel, out_shape=(shape((SLOTS, 3, CL, LANES)), shap...  21.5 us
    pallas_call x1, Pallas kernels, local(): pl.pallas_call(import_kernel, out_shape=shape((SLOTS, 5, CL, LANES)), in_...  20.7 us
    unnamed x16, local copies, waits for them, and re-layouts  4.51 us

profile of v1, /device:TPU:0, one launch (start us, length us, event | category | flops | bytes accessed | tf_op | source)
XLA Modules:
  0.0 111.9 jit_solution(1674764474703665426)
XLA Ops:
  1.3 0.0 copy-start.4
  1.3 0.6 copy-done.4
  1.9 0.0 copy-start
  1.9 0.9 copy-done
  2.8 0.0 copy-start.2
  2.8 0.8 copy-done.2
  3.6 0.0 copy-start.3
  3.6 0.8 copy-done.3
  4.3 0.0 copy-start.6
  4.3 20.7 %shard_map.95.places.fixed = f32[6,5,64,128]{3,2,1,0:T(8,128)S(1)} custom-call(f32[16]{0:T(128)S(1)} %copy-done.4, f32[3,64,128]{2,1,0:T(8,128)S(1)} %bitcast.5, f32[64,128]{1,0:T(8,128)S(1)} %copy-done.2, s32[64,128]{1,0:T(8,128)S(1)} %copy-done.3), custom_call_target="tpu_custom_call" | custom-call | tf_op jit(solution)/shard_map/pallas_call | solution.py:350
  25.1 0.0 copy-done.6
  25.1 0.0 copy-start.1
  25.1 19.1 %shard_map.96.partial = f32[6,3,64,128]{3,2,1,0:T(8,128)S(1)} custom-call(s32[2,256]{1,0:T(2,128)S(1)} %bitcast.9, s32[1]{0:T(128)S(6)} %copy.12.live, f32[6,5,64,128]{3,2,1,0:T(8,128)S(1)} %shard_map.95.places.fixed, f32[6,5,64,128]{3,2,1,0:T(8,128)S(1)} %shard_map.95.places.fixed), custom_call_target="tpu_custom_call" | custom-call | flops 503316480 | bytes 2097152 | tf_op jit(solution)/shard_map/pallas_call | solution.py:164
  44.2 0.0 copy-done.1
  44.2 21.5 %shard_map.97 = (f32[6,3,64,128]{3,2,1,0:T(8,128)S(1)}, f32[3,64,128]{2,1,0:T(8,128)S(1)}) custom-call(f32[6,3,64,128]{3,2,1,0:T(8,128)S(1)} %shard_map.96.partial, f32[6,5,64,128]{3,2,1,0:T(8,128)S(1)} %shard_map.95.places.fixed, f32[3,64,128]{2,1,0:T(8,128)S(1)} %bitcast.6), custom_call_target="tpu_custom_call" | custom-call | tf_op jit(solution)/shard_map/pallas_call | solution.py:359
  65.6 0.0 copy-start.5
  65.6 19.1 %shard_map.98.partial = f32[6,3,64,128]{3,2,1,0:T(8,128)S(1)} custom-call(s32[2,256]{1,0:T(2,128)S(1)} %bitcast.10, s32[1]{0:T(128)S(6)} %copy.12.live, f32[6,3,64,128]{3,2,1,0:T(8,128)S(1)} %get-tuple-element.6.places, f32[6,5,64,128]{3,2,1,0:T(8,128)S(1)} %shard_map.95.places.fixed), custom_call_target="tpu_custom_call" | custom-call | flops 503316480 | bytes 2097152 | tf_op jit(solution)/shard_map/pallas_call | solution.py:164
  84.8 0.0 copy-done.5
  84.8 25.6 %shard_map.99 = (f32[3,64,128]{2,1,0:T(8,128)S(1)}, f32[128,8,128]{2,1,0:T(8,128)S(1)}) custom-call(f32[6,3,64,128]{3,2,1,0:T(8,128)S(1)} %shard_map.98.partial, f32[6,5,64,128]{3,2,1,0:T(8,128)S(1)} %shard_map.95.places.fixed, f32[6,3,64,128]{3,2,1,0:T(8,128)S(1)} %get-tuple-element.6.places, f32[3,64,128]{2,1,0:T(8,128)S(1)} %get-tuple-element.7.moving, ...), custom_call_target="tpu_custom_call" | custom-call | tf_op jit(solution)/shard_map/pallas_call | solution.py:368
  110.4 0.6 copy.13
  111.1 0.8 copy.14
Async XLA Ops:
  1.3 0.7 copy-start.4
  1.9 0.9 copy-start
  2.8 0.8 copy-start.2
  3.6 0.8 copy-start.3
  4.3 20.7 %copy-start.6 = (s32[256,2]{0,1:T(2,128)S(1)}, s32[256,2]{0,1:T(2,128)}, u32[]{:S(2)}) copy-start(s32[256,2]{0,1:T(2,128)} %param.13) | copy-start | bytes 6148
  25.1 19.1 %copy-start.1 = (f32[64,3,128]{2,0,1:T(8,128)S(1)}, f32[64,3,128]{2,0,1:T(8,128)}, u32[]{:S(2)}) copy-start(f32[64,3,128]{2,0,1:T(8,128)} %param.9) | copy-start | bytes 294916
  65.6 19.2 %copy-start.5 = (s32[64,1]{0,1:T(1,128)S(1)}, s32[64,1]{0,1:T(1,128)}, u32[]{:S(2)}) copy-start(s32[64,1]{0,1:T(1,128)} %param.15) | copy-start | bytes 772

commit v2 on v1

--- a/solution.py
+++ b/solution.py
@@ -181,6 +181,7 @@
 
 
 VMEM = pl.BlockSpec(memory_space=pltpu.VMEM)
+HBM = pl.BlockSpec(memory_space=pltpu.HBM)
 SMEM = pl.BlockSpec(memory_space=pltpu.SMEM)
 BELOW, ABOVE = 4, 5
 
@@ -191,14 +192,25 @@
 
 def neighbours():
     z, y, x = here()
-    mine = y * 2 + x
-    partners = []
-    for dy, dx in ((0, 1), (1, 1), (1, 0)):
-        oy, ox = (1 - y if dy else y), (1 - x if dx else x)
-        partners.append(((z, oy, ox), oy * 2 + ox, mine))
-    partners.append(((lax.rem(z + 1, TOWERS), y, x), ABOVE, BELOW))
-    partners.append(((lax.rem(z + TOWERS - 1, TOWERS), y, x), BELOW, ABOVE))
-    return mine, partners
+    even = lax.rem(z, 2) == 0
+    step = 1 - 2 * lax.rem(z, 2)
+    pair = z + step
+    return dict(
+        core=(z, 1 - y, x),
+        pair=(pair, y, x),
+        cross=(pair, y, 1 - x),
+        ahead=(lax.rem(z + 2 * step + TOWERS, TOWERS), y, x),
+        behind=(lax.rem(z - 2 * step + TOWERS, TOWERS), y, x),
+        mine=y * 2 + x,
+        core_slot=(1 - y) * 2 + x,
+        plate_slot=y * 2 + 1 - x,
+        far_slot=(1 - y) * 2 + 1 - x,
+        pair_slot=ABOVE - lax.rem(z, 2),
+        other_slot=BELOW + lax.rem(z, 2),
+    )
+
+
+PARTNERS = ("core", "pair", "cross", "ahead", "behind")
 
 
 def greet(devices):
@@ -208,77 +220,124 @@
     return barrier
 
 
-def spread(buffer, send_sems, recv_sems):
-    mine, partners = neighbours()
-    copies = []
-    for k, (device, there, back) in enumerate(partners):
-        copy = pltpu.make_async_remote_copy(
-            buffer.at[mine], buffer.at[back], send_sems.at[k], recv_sems.at[back], device_id=device, device_id_type=MESH
-        )
+def remote(source, target, send_sems, recv_sems, way, chunk, device):
+    return pltpu.make_async_remote_copy(
+        source, target, send_sems.at[way, chunk], recv_sems.at[way, chunk], device_id=device, device_id_type=MESH
+    )
+
+
+def spread(n, buffer, count, send_sems, recv_sems, ready=None):
+    sent = []
+
+    def send(way, chunk, slot, there, name):
+        copy = remote(buffer.at[slot, chunk], buffer.at[there, chunk], send_sems, recv_sems, way, chunk, n[name])
         copy.start()
-        copies.append(copy)
-    for k, (device, there, back) in enumerate(partners):
-        pltpu.make_async_remote_copy(
-            buffer.at[there], buffer.at[there], send_sems.at[k], recv_sems.at[there], device_id=device, device_id_type=MESH
-        ).wait_recv()
-    for copy in copies:
+        sent.append(copy)
+
+    def arrive(way, chunk, slot):
+        remote(buffer.at[slot, chunk], buffer.at[slot, chunk], send_sems, recv_sems, way, chunk, n["core"]).wait_recv()
+
+    for c in range(count):
+        if ready:
+            ready(c)
+        send(1, c, n["mine"], n["other_slot"], "pair")
+        send(0, c, n["mine"], n["mine"], "core")
+    for c in range(count):
+        arrive(1, c, n["pair_slot"])
+        send(2, c, n["pair_slot"], n["mine"], "cross")
+        send(3, c, n["pair_slot"], n["other_slot"], "ahead")
+    for c in range(count):
+        arrive(2, c, n["plate_slot"])
+        send(4, c, n["plate_slot"], n["plate_slot"], "core")
+    for c in range(count):
+        arrive(0, c, n["core_slot"])
+        arrive(3, c, n["other_slot"])
+        arrive(4, c, n["far_slot"])
+    for copy in sent:
         copy.wait_send()
 
 
-def gather_forces(partial, landing, send_sems, recv_sems):
-    mine, partners = neighbours()
-    copies = []
-    for k, (device, there, back) in enumerate(partners):
-        copy = pltpu.make_async_remote_copy(
-            partial.at[there], landing.at[back], send_sems.at[k], recv_sems.at[back], device_id=device, device_id_type=MESH
-        )
+def gather_forces(n, partial, landing, send_sems, recv_sems):
+    sent = []
+
+    def send(way, chunk, source, name):
+        copy = remote(source, landing.at[way, chunk], send_sems, recv_sems, way, chunk, n[name])
         copy.start()
-        copies.append(copy)
-    total = [partial[mine, c] for c in range(3)]
-    for k, (device, there, back) in enumerate(partners):
-        pltpu.make_async_remote_copy(
-            landing.at[there], landing.at[there], send_sems.at[k], recv_sems.at[there], device_id=device, device_id_type=MESH
-        ).wait_recv()
-        total = [total[c] + landing[there, c] for c in range(3)]
-    for copy in copies:
-        copy.wait_send()
-    return total
-
-
-def import_kernel(radii, positions, charges, types, buffer, send_sems, recv_sems):
-    mine, partners = neighbours()
-    barrier = greet([p[0] for p in partners])
-    for c in range(3):
-        buffer[mine, c] = positions[c]
-    buffer[mine, 3] = charges[...]
-    kinds = types[...]
-    radius = jnp.zeros((CL, LANES), F32)
-    for kind in range(16):
-        radius = jnp.where(kinds == kind, radii[kind], radius)
-    buffer[mine, 4] = radius
-    pl.semaphore_wait(barrier, 5)
-    spread(buffer, send_sems, recv_sems)
+        sent.append(copy)
+
+    def arrive(way, chunk):
+        place = landing.at[way, chunk]
+        remote(place, place, send_sems, recv_sems, way, chunk, n["core"]).wait_recv()
+
+    for c in range(3):
+        send(0, c, partial.at[n["far_slot"], c], "core")
+        send(2, c, partial.at[n["other_slot"], c], "behind")
+    for c in range(3):
+        send(4, c, partial.at[n["core_slot"], c], "core")
+    for c in range(3):
+        arrive(0, c)
+        landing[5, c] = partial[n["plate_slot"], c] + landing[0, c]
+        send(1, c, landing.at[5, c], "cross")
+    for c in range(3):
+        arrive(1, c)
+        arrive(2, c)
+        landing[6, c] = partial[n["pair_slot"], c] + landing[1, c] + landing[2, c]
+        send(3, c, landing.at[6, c], "pair")
+    total = []
+    for c in range(3):
+        arrive(3, c)
+        arrive(4, c)
+        total.append(partial[n["mine"], c] + landing[3, c] + landing[4, c])
+    return total, sent
+
+
+def import_kernel(radii, positions, charges, types, buffer, kinds, table, load_sems, send_sems, recv_sems):
+    n = neighbours()
+    mine = n["mine"]
+    loads = [pltpu.make_async_copy(positions.at[c], buffer.at[mine, c], load_sems.at[c]) for c in range(3)]
+    loads.append(pltpu.make_async_copy(charges, buffer.at[mine, 3], load_sems.at[3]))
+    loads.append(pltpu.make_async_copy(types, kinds, load_sems.at[4]))
+    loads.append(pltpu.make_async_copy(radii, table, load_sems.at[5]))
+    for load in loads:
+        load.start()
+    barrier = greet([n[name] for name in PARTNERS])
+    pl.semaphore_wait(barrier, len(PARTNERS))
+
+    def ready(c):
+        loads[c].wait()
+        if c == 4:
+            loads[5].wait()
+            radius = jnp.zeros((CL, LANES), F32)
+            for kind in range(16):
+                radius = jnp.where(kinds[...] == kind, table[kind], radius)
+            buffer[mine, 4] = radius
+
+    spread(n, buffer, 5, send_sems, recv_sems, ready)
 
 
 def step_kernel(partial, fixed, velocities, places, moving, landing, send_sems, recv_sems, next_send, next_recv):
-    mine, partners = neighbours()
-    barrier = greet([p[0] for p in partners])
-    pl.semaphore_wait(barrier, 5)
-    forces = gather_forces(partial, landing, send_sems, recv_sems)
+    n = neighbours()
+    mine = n["mine"]
+    barrier = greet([n[name] for name in PARTNERS])
+    pl.semaphore_wait(barrier, len(PARTNERS))
+    forces, sent = gather_forces(n, partial, landing, send_sems, recv_sems)
     for c in range(3):
         speed = velocities[c] + time_step * forces[c]
         moving[c] = speed
         places[mine, c] = fixed[mine, c] + time_step * speed
-    spread(places, next_send, next_recv)
+    spread(n, places, 3, next_send, next_recv)
+    for copy in sent:
+        copy.wait_send()
 
 
 def last_kernel(
     partial, fixed, places, moving, destinations, forces_out, arrived, landing, slots, send_sems, recv_sems, out_sems, in_sems, own_sem
 ):
     z, y, x = here()
-    mine, partners = neighbours()
+    n = neighbours()
+    mine = n["mine"]
     others = [(lax.rem(z + k, TOWERS), y, x) for k in range(1, TOWERS)]
-    barrier = greet([p[0] for p in partners[:3]] + others)
+    barrier = greet([n["core"], n["cross"]] + others)
 
     row = jnp.broadcast_to(destinations[...].astype(F32), (CL, CL))
     r = lax.broadcasted_iota(jnp.int32, (CL, CL), 0)
@@ -288,8 +347,8 @@
     slot = row[0:1] * CAPACITY + rank
     select = (lax.broadcasted_iota(jnp.int32, (ARRIVING, CL), 0).astype(F32) == slot).astype(BF16)
 
-    pl.semaphore_wait(barrier, 3 + TOWERS - 1)
-    forces = gather_forces(partial, landing, send_sems, recv_sems)
+    pl.semaphore_wait(barrier, 2 + TOWERS - 1)
+    forces, sent = gather_forces(n, partial, landing, send_sems, recv_sems)
     carried = []
     speeds = []
     for k in range(3):
@@ -333,26 +392,28 @@
         receive(lax.rem(z + TOWERS - k, TOWERS)).wait_recv()
     for k in range(1, TOWERS):
         send(lax.rem(z + k, TOWERS)).wait_send()
+    for copy in sent:
+        copy.wait_send()
 
 
 def params(number):
     return pltpu.CompilerParams(collective_id=number, has_side_effects=True, vmem_limit_bytes=40 * 2**20)
 
 
-def dma(count):
-    return pltpu.SemaphoreType.DMA((count,))
+def dma(*counts):
+    return pltpu.SemaphoreType.DMA(counts)
 
 
 def local(positions, velocities, charges, atom_types, type_radius, tiles, tile_live, destinations):
     shape = functools.partial(jax.ShapeDtypeStruct, dtype=F32)
     pairs = tiles.T
-    landing = pltpu.VMEM((SLOTS, 3, CL, LANES), F32)
+    landing = pltpu.VMEM((7, 3, CL, LANES), F32)
     fixed = pl.pallas_call(
         import_kernel,
         out_shape=shape((SLOTS, 5, CL, LANES)),
-        in_specs=[SMEM, VMEM, VMEM, VMEM],
+        in_specs=[HBM] * 4,
         out_specs=VMEM,
-        scratch_shapes=[dma(5), dma(6)],
+        scratch_shapes=[pltpu.VMEM((CL, LANES), jnp.int32), pltpu.SMEM((16,), F32), dma(6), dma(5, 5), dma(5, 5)],
         compiler_params=params(0),
     )(type_radius, jnp.swapaxes(positions, 0, 1), charges, atom_types)
     partial = tile_forces(pairs, tile_live, fixed, fixed)
@@ -361,7 +422,7 @@
         out_shape=(shape((SLOTS, 3, CL, LANES)), shape((3, CL, LANES))),
         in_specs=[VMEM] * 3,
         out_specs=(VMEM, VMEM),
-        scratch_shapes=[landing, dma(5), dma(6), dma(5), dma(6)],
+        scratch_shapes=[landing, dma(5, 3), dma(5, 3), dma(5, 3), dma(5, 3)],
         compiler_params=params(1),
     )(partial, fixed, jnp.swapaxes(velocities, 0, 1))
     partial = tile_forces(pairs, tile_live, places, fixed)
@@ -373,8 +434,8 @@
         scratch_shapes=[
             landing,
             pltpu.VMEM((ARRIVING, 8, LANES), F32),
-            dma(5),
-            dma(6),
+            dma(5, 3),
+            dma(5, 3),
             dma(TOWERS),
             dma(TOWERS),
             pltpu.SemaphoreType.DMA,

time: 113 us -> 102 us (0.903)
  Pallas kernels: 106 us -> 96.1 us
    pallas_call x2, Pallas kernels: 38.2 us -> 18.5 us  [tile_forces(): pl.pallas_call(tile_kernel, out_shape=jax.ShapeDtypeStruct((SLOTS, 3, CL,...]
    pallas_call x1, Pallas kernels: 21.5 us -> 30 us  [local(): pl.pallas_call(step_kernel, out_shape=(shape((SLOTS, 3, CL, LANES)), shap...]
    pallas_call x1, Pallas kernels: 25.6 us -> 30.1 us  [local(): pl.pallas_call(last_kernel, out_shape=(shape((3, CL, LANES)), shape((ARRI...]
    pallas_call x1, Pallas kernels: 20.7 us -> 17.5 us  [local(): pl.pallas_call(import_kernel, out_shape=shape((SLOTS, 5, CL, LANES)), in_...]
where the time goes in v2:
time: 102 us
  Pallas kernels  96.1 us (94%)
  local copies, waits for them, and re-layouts  4.51 us (4%)
  between operations  1.37 us (1%)
    pallas_call x1, Pallas kernels, local(): pl.pallas_call(last_kernel, out_shape=(shape((3, CL, LANES)), shape((ARRI...  30.1 us
    pallas_call x1, Pallas kernels, local(): pl.pallas_call(step_kernel, out_shape=(shape((SLOTS, 3, CL, LANES)), shap...  30 us
    pallas_call x2, Pallas kernels, tile_forces(): pl.pallas_call(tile_kernel, out_shape=jax.ShapeDtypeStruct((SLOTS, 3, CL,...  18.5 us
    pallas_call x1, Pallas kernels, local(): pl.pallas_call(import_kernel, out_shape=shape((SLOTS, 5, CL, LANES)), in_...  17.5 us
    unnamed x16, local copies, waits for them, and re-layouts  4.51 us

profile of v2, /device:TPU:0, one launch (start us, length us, event | category | flops | bytes accessed | tf_op | source)
XLA Modules:
  0.0 102.0 jit_solution(17927616186547438415)
XLA Ops:
  1.3 0.0 copy-start.4
  1.3 0.6 copy-done.4
  1.9 0.0 copy-start
  1.9 0.9 copy-done
  2.8 0.0 copy-start.2
  2.8 0.8 copy-done.2
  3.6 0.0 copy-start.3
  3.6 0.8 copy-done.3
  4.3 0.0 copy-start.6
  4.3 17.5 %shard_map.95.places.fixed = f32[6,5,64,128]{3,2,1,0:T(8,128)S(1)} custom-call(f32[16]{0:T(128)S(1)} %copy-done.4, f32[3,64,128]{2,1,0:T(8,128)S(1)} %bitcast.5, f32[64,128]{1,0:T(8,128)S(1)} %copy-done.2, s32[64,128]{1,0:T(8,128)S(1)} %copy-done.3), custom_call_target="tpu_custom_call" | custom-call | tf_op jit(solution)/shard_map/pallas_call | solution.py:411
  21.8 0.0 copy-done.6
  21.8 0.0 copy-start.1
  21.9 9.2 %shard_map.96.partial = f32[6,3,64,128]{3,2,1,0:T(8,128)S(1)} custom-call(s32[2,256]{1,0:T(2,128)S(1)} %bitcast.9, s32[1]{0:T(128)S(6)} %copy.12.live, f32[6,5,64,128]{3,2,1,0:T(8,128)S(1)} %shard_map.95.places.fixed, f32[6,5,64,128]{3,2,1,0:T(8,128)S(1)} %shard_map.95.places.fixed), custom_call_target="tpu_custom_call" | custom-call | flops 503316480 | bytes 2097152 | tf_op jit(solution)/shard_map/pallas_call | solution.py:164
  31.1 0.0 copy-done.1
  31.1 30.0 %shard_map.97 = (f32[6,3,64,128]{3,2,1,0:T(8,128)S(1)}, f32[3,64,128]{2,1,0:T(8,128)S(1)}) custom-call(f32[6,3,64,128]{3,2,1,0:T(8,128)S(1)} %shard_map.96.partial, f32[6,5,64,128]{3,2,1,0:T(8,128)S(1)} %shard_map.95.places.fixed, f32[3,64,128]{2,1,0:T(8,128)S(1)} %bitcast.6), custom_call_target="tpu_custom_call" | custom-call | tf_op jit(solution)/shard_map/pallas_call | solution.py:420
  61.1 0.0 copy-start.5
  61.1 9.3 %shard_map.98.partial = f32[6,3,64,128]{3,2,1,0:T(8,128)S(1)} custom-call(s32[2,256]{1,0:T(2,128)S(1)} %bitcast.10, s32[1]{0:T(128)S(6)} %copy.12.live, f32[6,3,64,128]{3,2,1,0:T(8,128)S(1)} %get-tuple-element.6.places, f32[6,5,64,128]{3,2,1,0:T(8,128)S(1)} %shard_map.95.places.fixed), custom_call_target="tpu_custom_call" | custom-call | flops 503316480 | bytes 2097152 | tf_op jit(solution)/shard_map/pallas_call | solution.py:164
  70.4 0.0 copy-done.5
  70.4 30.1 %shard_map.99 = (f32[3,64,128]{2,1,0:T(8,128)S(1)}, f32[128,8,128]{2,1,0:T(8,128)S(1)}) custom-call(f32[6,3,64,128]{3,2,1,0:T(8,128)S(1)} %shard_map.98.partial, f32[6,5,64,128]{3,2,1,0:T(8,128)S(1)} %shard_map.95.places.fixed, f32[6,3,64,128]{3,2,1,0:T(8,128)S(1)} %get-tuple-element.6.places, f32[3,64,128]{2,1,0:T(8,128)S(1)} %get-tuple-element.7.moving, ...), custom_call_target="tpu_custom_call" | custom-call | tf_op jit(solution)/shard_map/pallas_call | solution.py:429
  100.6 0.6 copy.13
  101.2 0.8 copy.14
Async XLA Ops:
  1.3 0.7 copy-start.4
  1.9 0.9 copy-start
  2.8 0.8 copy-start.2
  3.6 0.8 copy-start.3
  4.3 17.5 %copy-start.6 = (s32[256,2]{0,1:T(2,128)S(1)}, s32[256,2]{0,1:T(2,128)}, u32[]{:S(2)}) copy-start(s32[256,2]{0,1:T(2,128)} %param.13) | copy-start | bytes 6148
  21.8 9.2 %copy-start.1 = (f32[64,3,128]{2,0,1:T(8,128)S(1)}, f32[64,3,128]{2,0,1:T(8,128)}, u32[]{:S(2)}) copy-start(f32[64,3,128]{2,0,1:T(8,128)} %param.9) | copy-start | bytes 294916
  61.1 9.3 %copy-start.5 = (s32[64,1]{0,1:T(1,128)S(1)}, s32[64,1]{0,1:T(1,128)}, u32[]{:S(2)}) copy-start(s32[64,1]{0,1:T(1,128)} %param.15) | copy-start | bytes 772

commit v3 on v2

v3 whole, which is shorter than its diff:
```python
import functools

import jax
import jax.numpy as jnp
from jax import lax
from jax.experimental import pallas as pl
from jax.experimental.pallas import tpu as pltpu
from jax.sharding import PartitionSpec as P

coulomb = 0.3
time_step = 0.05

MESH = pl.DeviceIdType.MESH
F32 = jnp.float32
BF16 = jnp.bfloat16

CL = 64
LANES = 128
SLOTS = 6
ROWS = SLOTS * CL
CAPACITY = 4
TILES = 256
TOWERS = 32
ARRIVING = TOWERS * CAPACITY
UNROLL = 16
CENTER = 2.0
PLANES = 32
CHANNELS = 8
RADIUS, CHARGE = 3, 4


def split(x):
    high = x.astype(BF16).astype(F32)
    rest = x - high
    middle = rest.astype(BF16).astype(F32)
    return high, middle, rest - middle


def tile_kernel(tiles, live, blocks, out, planes, totals, store_a, store_b):
    line = lax.broadcasted_iota(jnp.int32, (8, LANES), 0)
    upper = line < 4
    center = jnp.where(line < 3, CENTER, 0.0).astype(F32)
    zero = jnp.zeros((8, LANES), F32)

    def prepare(step, carry):
        slot, inner = step // (CL // 8), step % (CL // 8)
        for k in range(8):
            first = pl.multiple_of(slot * (CHANNELS * CL) + inner * 8, 8) + k
            to = pl.multiple_of(step * 256, 256) + k * 32
            loaded = blocks[pl.ds(first, 8, stride=CL), :] - center
            twice = jnp.where(upper, loaded, pltpu.roll(loaded, 4, 0))
            charge = jnp.broadcast_to(loaded[4:5, :], (8, LANES))
            high, middle, low = split(twice)
            planes[pl.ds(to, 8), :] = jnp.where(upper, high, middle)
            planes[pl.ds(to + 8, 8), :] = jnp.where(upper, low, high)
            square = twice * twice
            square = square + pltpu.roll(square, 2, 0)
            square = 0.5 * (square + pltpu.roll(square, 1, 0))
            high, middle, low = split(square)
            parts = jnp.where(line == 0, high, jnp.where(line == 1, middle, low))
            planes[pl.ds(to + 16, 8), :] = jnp.where(line < 3, parts, jnp.where((line == 3) | (line == 7), 0.0, 1.0))
            weighted = jnp.where((line == 3) | (line == 7), 1.0, twice) * charge
            high = weighted.astype(BF16).astype(F32)
            planes[pl.ds(to + 24, 8), :] = jnp.where(upper, high, weighted - high)
            totals[pl.ds(pl.multiple_of(step * 64, 64) + k * 8, 8), :] = zero
        return carry

    lax.fori_loop(0, ROWS // 8, prepare, 0)

    sign = jnp.where(line % 4 == 3, 1.0, -1.0).astype(F32)
    live_count = live[0]

    def eight(plane, row):
        return planes[pl.ds(pl.multiple_of(row * 32, 32) + plane * 8, 8), :]

    blank = jnp.zeros((32, LANES), F32)

    def powers_of(group, pair, store):
        lefts, rights = [], []
        for v in range(2):
            a, b = tiles[0, group * UNROLL + 2 * pair + v], tiles[1, group * UNROLL + 2 * pair + v]
            near = eight(0, a) * sign
            lefts += [near, near, eight(1, a) * sign, eight(2, a)]
            r0, r1, r2 = eight(0, b), eight(1, b), eight(2, b)
            rights.append(
                jnp.concatenate([r0, pltpu.roll(r0, 4, 0), pltpu.roll(r1, 4, 0), pltpu.roll(r2, 4, 0)], axis=0)
            )
        left = jnp.concatenate(lefts, axis=0)
        right = jnp.concatenate(
            [jnp.concatenate([rights[0], blank], axis=1), jnp.concatenate([blank, rights[1]], axis=1)], axis=0
        )
        half_dist = lax.dot_general(
            left.astype(BF16), right.astype(BF16), (((0,), (0,)), ((), ())), preferred_element_type=F32
        )
        root = lax.rsqrt(half_dist)
        power = root * root * root
        high = power.astype(BF16)
        store[pair, 0:128, :] = high
        store[pair, 128:256, :] = (power - high.astype(F32)).astype(BF16)

    def sums_of(group, pair, store, sums):
        ids = [(tiles[0, group * UNROLL + 2 * pair + v], tiles[1, group * UNROLL + 2 * pair + v]) for v in range(2)]
        active = [jnp.where(group * UNROLL + 2 * pair + v < live_count, 1.0, 0.0).astype(F32) for v in range(2)]
        from_a = jnp.concatenate([eight(3, ids[v][0]) * active[v] for v in range(2)], axis=0).astype(BF16)
        from_b = jnp.concatenate([eight(3, ids[v][1]) * active[v] for v in range(2)], axis=0).astype(BF16)
        on_right = jnp.dot(jnp.concatenate([from_a, from_a], axis=1), store[pair], preferred_element_type=F32)
        across = jnp.concatenate(
            [
                jnp.concatenate([store[pair, 0:128, 0:128], store[pair, 128:256, 0:128]], axis=1),
                jnp.concatenate([store[pair, 0:128, 128:256], store[pair, 128:256, 128:256]], axis=1),
            ],
            axis=0,
        )
        on_left = lax.dot_general(
            jnp.concatenate([from_b, from_b], axis=1), across, (((1,), (1,)), ((), ())), preferred_element_type=F32
        )
        sums.append((ids[0][0], on_left[0:8, :LANES]))
        sums.append((ids[0][1], on_right[0:8, :LANES]))
        sums.append((ids[1][0], on_left[8:16, LANES:]))
        sums.append((ids[1][1], on_right[8:16, LANES:]))

    def add(sums):
        for row, value in sums:
            at = pl.ds(pl.multiple_of(row * 8, 8), 8)
            totals[at, :] = totals[at, :] + value

    half_group = UNROLL // 2
    for pair in range(half_group):
        powers_of(0, pair, store_a)

    def two_groups(step, carry):
        group = 2 * step
        for now, later, shift in ((store_a, store_b, 1), (store_b, store_a, 2)):
            sums = []
            for pair in range(half_group):
                powers_of(jnp.minimum(group + shift, TILES // UNROLL - 1), pair, later)
                sums_of(group + shift - 1, pair, now, sums)
            add(sums)
        return carry

    lax.fori_loop(0, (live_count + 2 * UNROLL - 1) // (2 * UNROLL), two_groups, 0)

    factor = coulomb * 0.5**1.5

    def finish(group, carry):
        slot, inner = group // (CL // 8), group % (CL // 8)
        rows = pl.ds(pl.multiple_of(inner * 8, 8), 8)

        def plane(c):
            return blocks[pl.ds(pl.multiple_of(slot * (CHANNELS * CL) + c * CL + inner * 8, 8), 8), :]

        def summed(channel):
            first = pl.multiple_of(group * 64, 64) + channel
            return totals[pl.ds(first, 8, stride=8), :] + totals[pl.ds(first + 4, 8, stride=8), :]

        scale = factor * plane(4)
        whole = summed(3)
        for c in range(3):
            out[slot, c, rows, :] = scale * ((plane(c) - CENTER) * whole - summed(c))
        return carry

    lax.fori_loop(0, ROWS // 8, finish, 0)


def tile_forces(tiles, live, blocks):
    return pl.pallas_call(
        tile_kernel,
        out_shape=jax.ShapeDtypeStruct((SLOTS, 3, CL, LANES), F32),
        in_specs=[
            pl.BlockSpec(memory_space=pltpu.SMEM),
            pl.BlockSpec(memory_space=pltpu.SMEM),
            pl.BlockSpec(memory_space=pltpu.VMEM),
        ],
        out_specs=pl.BlockSpec(memory_space=pltpu.VMEM),
        scratch_shapes=[
            pltpu.VMEM((PLANES * ROWS, LANES), F32),
            pltpu.VMEM((ROWS * 8, LANES), F32),
            pltpu.VMEM((UNROLL // 2, 256, 256), BF16),
            pltpu.VMEM((UNROLL // 2, 256, 256), BF16),
        ],
        compiler_params=pltpu.CompilerParams(vmem_limit_bytes=40 * 2**20),
        cost_estimate=pl.CostEstimate(flops=256 * 128 * 128 * 120, bytes_accessed=2 * 2**20, transcendentals=256 * 128 * 128),
    )(tiles, live, blocks.reshape(SLOTS * CHANNELS * CL, LANES))


VMEM = pl.BlockSpec(memory_space=pltpu.VMEM)
HBM = pl.BlockSpec(memory_space=pltpu.HBM)
SMEM = pl.BlockSpec(memory_space=pltpu.SMEM)
BELOW, ABOVE = 4, 5


def here():
    return lax.axis_index("gz"), lax.axis_index("gy"), lax.axis_index("gx")


def neighbours():
    z, y, x = here()
    even = lax.rem(z, 2) == 0
    step = 1 - 2 * lax.rem(z, 2)
    pair = z + step
    return dict(
        core=(z, 1 - y, x),
        pair=(pair, y, x),
        cross=(pair, y, 1 - x),
        ahead=(lax.rem(z + 2 * step + TOWERS, TOWERS), y, x),
        behind=(lax.rem(z - 2 * step + TOWERS, TOWERS), y, x),
        mine=y * 2 + x,
        core_slot=(1 - y) * 2 + x,
        plate_slot=y * 2 + 1 - x,
        far_slot=(1 - y) * 2 + 1 - x,
        pair_slot=ABOVE - lax.rem(z, 2),
        other_slot=BELOW + lax.rem(z, 2),
    )


PARTNERS = ("core", "pair", "cross", "ahead", "behind")


def greet(devices):
    barrier = pltpu.get_barrier_semaphore()
    for device in devices:
        pl.semaphore_signal(barrier, inc=1, device_id=device, device_id_type=MESH)
    return barrier


def remote(source, target, send_sems, recv_sems, way, chunk, device):
    return pltpu.make_async_remote_copy(
        source, target, send_sems.at[way, chunk], recv_sems.at[way, chunk], device_id=device, device_id_type=MESH
    )


def spread(n, buffer, channels, send_sems, recv_sems, ready):
    sent = []

    def send(way, chunk, slot, there, name):
        copy = remote(buffer.at[slot, chunk], buffer.at[there, chunk], send_sems, recv_sems, way, chunk, n[name])
        copy.start()
        sent.append(copy)

    def arrive(way, chunk, slot):
        remote(buffer.at[slot, chunk], buffer.at[slot, chunk], send_sems, recv_sems, way, chunk, n["core"]).wait_recv()

    for c in channels:
        ready(c)
        send(1, c, n["mine"], n["other_slot"], "pair")
        send(0, c, n["mine"], n["mine"], "core")
    for c in channels:
        arrive(1, c, n["pair_slot"])
        send(2, c, n["pair_slot"], n["mine"], "cross")
        send(3, c, n["pair_slot"], n["other_slot"], "ahead")
    for c in channels:
        arrive(2, c, n["plate_slot"])
        send(4, c, n["plate_slot"], n["plate_slot"], "core")
    for c in channels:
        arrive(0, c, n["core_slot"])
        arrive(3, c, n["other_slot"])
        arrive(4, c, n["far_slot"])
    for copy in sent:
        copy.wait_send()


def gather_forces(n, partial, landing, send_sems, recv_sems):
    sent = []

    def send(way, chunk, source, name):
        copy = remote(source, landing.at[way, chunk], send_sems, recv_sems, way, chunk, n[name])
        copy.start()
        sent.append(copy)

    def arrive(way, chunk):
        place = landing.at[way, chunk]
        remote(place, place, send_sems, recv_sems, way, chunk, n["core"]).wait_recv()

    for c in range(3):
        send(0, c, partial.at[n["far_slot"], c], "core")
        send(2, c, partial.at[n["other_slot"], c], "behind")
    for c in range(3):
        send(4, c, partial.at[n["core_slot"], c], "core")
    for c in range(3):
        arrive(0, c)
        landing[5, c] = partial[n["plate_slot"], c] + landing[0, c]
        send(1, c, landing.at[5, c], "cross")
    for c in range(3):
        arrive(1, c)
        arrive(2, c)
        landing[6, c] = partial[n["pair_slot"], c] + landing[1, c] + landing[2, c]
        send(3, c, landing.at[6, c], "pair")

    def total(c):
        arrive(3, c)
        arrive(4, c)
        return partial[n["mine"], c] + landing[3, c] + landing[4, c]

    return total, sent


def import_kernel(radii, positions, charges, types, buffer, kinds, table, load_sems, send_sems, recv_sems):
    n = neighbours()
    mine = n["mine"]
    loads = [pltpu.make_async_copy(positions.at[c], buffer.at[mine, c], load_sems.at[c]) for c in range(3)]
    loads.append(pltpu.make_async_copy(types, kinds, load_sems.at[3]))
    loads.append(pltpu.make_async_copy(charges, buffer.at[mine, CHARGE], load_sems.at[4]))
    loads.append(pltpu.make_async_copy(radii, table, load_sems.at[5]))
    for load in loads:
        load.start()
    barrier = greet([n[name] for name in PARTNERS])
    pl.semaphore_wait(barrier, len(PARTNERS))

    def ready(c):
        loads[c].wait()
        if c == RADIUS:
            loads[5].wait()
            radius = jnp.zeros((CL, LANES), F32)
            for kind in range(16):
                radius = jnp.where(kinds[...] == kind, table[kind], radius)
            buffer[mine, RADIUS] = radius

    spread(n, buffer, (0, 1, 2, CHARGE, RADIUS), send_sems, recv_sems, ready)


def step_kernel(partial, fixed, velocities, places, moving, landing, send_sems, recv_sems, next_send, next_recv):
    n = neighbours()
    mine = n["mine"]
    barrier = greet([n[name] for name in PARTNERS])
    pl.semaphore_wait(barrier, len(PARTNERS))
    force, sent = gather_forces(n, partial, landing, send_sems, recv_sems)

    def ready(c):
        speed = velocities[c] + time_step * force(c)
        moving[c] = speed
        places[mine, c] = fixed[mine, c] + time_step * speed

    for slot in range(SLOTS):
        for c in (RADIUS, CHARGE):
            places[slot, c] = fixed[slot, c]
    spread(n, places, range(3), next_send, next_recv, ready)
    for copy in sent:
        copy.wait_send()


def last_kernel(
    partial, places, moving, destinations, forces_out, arrived, landing, slots, send_sems, recv_sems, out_sems, in_sems, own_sem
):
    z, y, x = here()
    n = neighbours()
    mine = n["mine"]
    others = [(lax.rem(z + k, TOWERS), y, x) for k in range(1, TOWERS)]
    barrier = greet([n["core"], n["cross"]] + others)

    row = jnp.broadcast_to(destinations[...].astype(F32), (CL, CL))
    r = lax.broadcasted_iota(jnp.int32, (CL, CL), 0)
    c = lax.broadcasted_iota(jnp.int32, (CL, CL), 1)
    column = jnp.sum(jnp.where(r == c, row, 0.0), axis=1, keepdims=True)
    rank = jnp.sum(jnp.where((column == row) & (r < c), 1.0, 0.0), axis=0, keepdims=True)
    slot = row[0:1] * CAPACITY + rank
    select = (lax.broadcasted_iota(jnp.int32, (ARRIVING, CL), 0).astype(F32) == slot).astype(BF16)

    pl.semaphore_wait(barrier, 2 + TOWERS - 1)
    force, sent = gather_forces(n, partial, landing, send_sems, recv_sems)
    carried = []
    speeds = []
    for k in range(3):
        total = force(k)
        forces_out[k] = total
        speed = moving[k] + time_step * total
        speeds.append(speed)
        carried.append(places[mine, k] + time_step * speed)
    carried = carried + speeds + [places[mine, CHARGE], places[mine, RADIUS]]
    for k, value in enumerate(carried):
        parts = split(value)
        slots[:, k, :] = sum(jnp.dot(select, part.astype(BF16), preferred_element_type=F32) for part in reversed(parts))

    def send(tower):
        return pltpu.make_async_remote_copy(
            slots.at[pl.ds(tower * CAPACITY, CAPACITY)],
            arrived.at[pl.ds(z * CAPACITY, CAPACITY)],
            out_sems.at[tower],
            in_sems.at[z],
            device_id=(tower, y, x),
            device_id_type=MESH,
        )

    def receive(tower):
        return pltpu.make_async_remote_copy(
            slots.at[pl.ds(tower * CAPACITY, CAPACITY)],
            arrived.at[pl.ds(tower * CAPACITY, CAPACITY)],
            out_sems.at[tower],
            in_sems.at[tower],
            device_id=(tower, y, x),
            device_id_type=MESH,
        )

    for k in range(1, TOWERS):
        send(lax.rem(z + k, TOWERS)).start()
    own = pltpu.make_async_copy(
        slots.at[pl.ds(z * CAPACITY, CAPACITY)], arrived.at[pl.ds(z * CAPACITY, CAPACITY)], own_sem
    )
    own.start()
    own.wait()
    for k in range(1, TOWERS):
        receive(lax.rem(z + TOWERS - k, TOWERS)).wait_recv()
    for k in range(1, TOWERS):
        send(lax.rem(z + k, TOWERS)).wait_send()
    for copy in sent:
        copy.wait_send()


def params(number):
    return pltpu.CompilerParams(collective_id=number, has_side_effects=True, vmem_limit_bytes=40 * 2**20)


def dma(*counts):
    return pltpu.SemaphoreType.DMA(counts)


def local(positions, velocities, charges, atom_types, type_radius, tiles, tile_live, destinations):
    held = functools.partial(pltpu.with_memory_space_constraint, memory_space=pltpu.HBM)
    shape = functools.partial(jax.ShapeDtypeStruct, dtype=F32)
    pairs = tiles.T
    landing = pltpu.VMEM((7, 3, CL, LANES), F32)
    fixed = pl.pallas_call(
        import_kernel,
        out_shape=shape((SLOTS, CHANNELS, CL, LANES)),
        in_specs=[HBM] * 4,
        out_specs=VMEM,
        scratch_shapes=[pltpu.VMEM((CL, LANES), jnp.int32), pltpu.SMEM((16,), F32), dma(6), dma(5, 5), dma(5, 5)],
        compiler_params=params(0),
    )(*(held(v) for v in (type_radius, jnp.swapaxes(positions, 0, 1), charges, atom_types)))
    partial = tile_forces(pairs, tile_live, fixed)
    places, moving = pl.pallas_call(
        step_kernel,
        out_shape=(shape((SLOTS, CHANNELS, CL, LANES)), shape((3, CL, LANES))),
        in_specs=[VMEM] * 3,
        out_specs=(VMEM, VMEM),
        scratch_shapes=[landing, dma(5, 3), dma(5, 3), dma(5, 3), dma(5, 3)],
        compiler_params=params(1),
    )(partial, fixed, jnp.swapaxes(velocities, 0, 1))
    partial = tile_forces(pairs, tile_live, places)
    forces, arrived = pl.pallas_call(
        last_kernel,
        out_shape=(shape((3, CL, LANES)), shape((ARRIVING, 8, LANES))),
        in_specs=[VMEM] * 4,
        out_specs=(VMEM, VMEM),
        scratch_shapes=[
            landing,
            pltpu.VMEM((ARRIVING, 8, LANES), F32),
            dma(5, 3),
            dma(5, 3),
            dma(TOWERS),
            dma(TOWERS),
            pltpu.SemaphoreType.DMA,
        ],
        compiler_params=params(2),
    )(partial, places, moving, destinations.T)
    return jnp.swapaxes(forces, 0, 1), arrived


def solution(mesh):
    home = ("gz", "gy", "gx")
    placed = (
        P(home, None, None),
        P(home, None, None),
        P(home, None),
        P(home, None),
        P(),
        P(home, None),
        P(home),
        P(home, None),
    )
    return jax.shard_map(
        local,
        mesh=mesh,
        in_specs=placed,
        out_specs=(P(home, None, None), P(home, None, None)),
        check_vma=False,
    )
```

time: 102 us -> 86.5 us (0.85)
  Pallas kernels: 96.1 us -> 83.4 us
  local copies, waits for them, and re-layouts: 4.51 us -> 1.45 us
    pallas_call x2, Pallas kernels: 47.5 us -> 35.5 us  [the longest x1 18.1 us: local(): pl.pallas_call(step_kernel, out_shape=(shape((SLOTS, CHANNELS, CL, LANES)...]
    pallas_call x1, Pallas kernels: 30.1 us -> 19.9 us  [local(): pl.pallas_call(last_kernel, out_shape=(shape((3, CL, LANES)), shape((ARRI...]
    pallas_call x2, Pallas kernels: 18.5 us -> 27.9 us  [tile_forces(): pl.pallas_call(tile_kernel, out_shape=jax.ShapeDtypeStruct((SLOTS, 3, CL,...]
    unnamed x16 -> x8, local copies, waits for them, and re-layouts: 4.51 us -> 1.45 us
where the time goes in v3:
time: 86.5 us; the launch traced here: 86.2 us
  Pallas kernels  83.4 us (96%)
  local copies, waits for them, and re-layouts  1.45 us (2%)
  between operations  1.38 us (2%)
    pallas_call x2, Pallas kernels, tile_forces(): pl.pallas_call(tile_kernel, out_shape=jax.ShapeDtypeStruct((SLOTS, 3, CL,...  27.9 us
    pallas_call x1, Pallas kernels, local(): pl.pallas_call(last_kernel, out_shape=(shape((3, CL, LANES)), shape((ARRI...  19.9 us
    pallas_call x1, Pallas kernels, local(): pl.pallas_call(step_kernel, out_shape=(shape((SLOTS, CHANNELS, CL, LANES)...  18.1 us
    pallas_call x1, Pallas kernels, local(): pl.pallas_call(import_kernel, out_shape=shape((SLOTS, CHANNELS, CL, LANES...  17.4 us

profile of v3, /device:TPU:0, one launch (start us, length us, event | category | flops | bytes accessed | tf_op | source)
XLA Modules:
  0.0 86.2 jit_solution(1470947030414845875)
XLA Ops:
  0.6 0.0 copy-start.2
  1.3 17.4 %shard_map.95.fixed = f32[6,8,64,128]{3,2,1,0:T(8,128)S(1)} custom-call(f32[16]{0:T(128)} %radii.1, f32[3,64,128]{2,1,0:T(8,128)} %bitcast.14, f32[64,128]{1,0:T(8,128)} %charges.1, s32[64,128]{1,0:T(8,128)} %types.1), custom_call_target="tpu_custom_call" | custom-call | tf_op jit(solution)/shard_map/pallas_call | solution.py:421
  18.7 0.0 copy-done.2
  18.7 0.0 copy-start
  18.7 14.0 %shard_map.96.partial = f32[6,3,64,128]{3,2,1,0:T(8,128)S(1)} custom-call(s32[2,256]{1,0:T(2,128)S(1)} %bitcast.12, s32[1]{0:T(128)S(6)} %copy.12.live, f32[3072,128]{1,0:T(8,128)S(1)} %bitcast.7), custom_call_target="tpu_custom_call" | custom-call | flops 503316480 | bytes 2097152 | tf_op jit(solution)/shard_map/pallas_call | solution.py:166
  32.7 0.0 copy-done
  32.7 18.1 %shard_map.97 = (f32[6,8,64,128]{3,2,1,0:T(8,128)S(1)}, f32[3,64,128]{2,1,0:T(8,128)S(1)}) custom-call(f32[6,3,64,128]{3,2,1,0:T(8,128)S(1)} %shard_map.96.partial, f32[6,8,64,128]{3,2,1,0:T(8,128)S(1)} %shard_map.95.fixed, f32[3,64,128]{2,1,0:T(8,128)S(1)} %bitcast.9), custom_call_target="tpu_custom_call" | custom-call | tf_op jit(solution)/shard_map/pallas_call | solution.py:430
  50.8 0.0 copy-start.1
  50.9 14.0 %shard_map.98.partial = f32[6,3,64,128]{3,2,1,0:T(8,128)S(1)} custom-call(s32[2,256]{1,0:T(2,128)S(1)} %bitcast.13, s32[1]{0:T(128)S(6)} %copy.12.live, f32[3072,128]{1,0:T(8,128)S(1)} %bitcast.8), custom_call_target="tpu_custom_call" | custom-call | flops 503316480 | bytes 2097152 | tf_op jit(solution)/shard_map/pallas_call | solution.py:166
  64.8 0.0 copy-done.1
  64.8 19.9 %shard_map.99 = (f32[3,64,128]{2,1,0:T(8,128)S(1)}, f32[128,8,128]{2,1,0:T(8,128)S(1)}) custom-call(f32[6,3,64,128]{3,2,1,0:T(8,128)S(1)} %shard_map.98.partial, f32[6,8,64,128]{3,2,1,0:T(8,128)S(1)} %get-tuple-element.6.places, f32[3,64,128]{2,1,0:T(8,128)S(1)} %get-tuple-element.7.moving, s32[1,64]{1,0:T(1,128)S(1)} %bitcast.11), custom_call_target="tpu_custom_call" | custom-call | tf_op jit(solution)/shard_map/pallas_call | solution.py:439
  84.8 0.6 copy.13
  85.4 0.8 copy.14
Async XLA Ops:
  0.6 18.1 %copy-start.2 = (s32[256,2]{0,1:T(2,128)S(1)}, s32[256,2]{0,1:T(2,128)}, u32[]{:S(2)}) copy-start(s32[256,2]{0,1:T(2,128)} %param.13) | copy-start | bytes 6148
  18.7 14.0 %copy-start = (f32[64,3,128]{2,0,1:T(8,128)S(1)}, f32[64,3,128]{2,0,1:T(8,128)}, u32[]{:S(2)}) copy-start(f32[64,3,128]{2,0,1:T(8,128)} %param.9) | copy-start | bytes 294916
  50.8 14.0 %copy-start.1 = (s32[64,1]{0,1:T(1,128)S(1)}, s32[64,1]{0,1:T(1,128)}, u32[]{:S(2)}) copy-start(s32[64,1]{0,1:T(1,128)} %param.15) | copy-start | bytes 772

commit v4 on v3

--- a/solution.py
+++ b/solution.py
@@ -36,36 +36,15 @@
     return high, middle, rest - middle
 
 
-def tile_kernel(tiles, live, blocks, out, planes, totals, store_a, store_b):
+def tile_kernel(tiles, live, blocks, planes, out, totals, store_a, store_b):
     line = lax.broadcasted_iota(jnp.int32, (8, LANES), 0)
-    upper = line < 4
-    center = jnp.where(line < 3, CENTER, 0.0).astype(F32)
-    zero = jnp.zeros((8, LANES), F32)
-
-    def prepare(step, carry):
-        slot, inner = step // (CL // 8), step % (CL // 8)
+
+    def clear(step, carry):
         for k in range(8):
-            first = pl.multiple_of(slot * (CHANNELS * CL) + inner * 8, 8) + k
-            to = pl.multiple_of(step * 256, 256) + k * 32
-            loaded = blocks[pl.ds(first, 8, stride=CL), :] - center
-            twice = jnp.where(upper, loaded, pltpu.roll(loaded, 4, 0))
-            charge = jnp.broadcast_to(loaded[4:5, :], (8, LANES))
-            high, middle, low = split(twice)
-            planes[pl.ds(to, 8), :] = jnp.where(upper, high, middle)
-            planes[pl.ds(to + 8, 8), :] = jnp.where(upper, low, high)
-            square = twice * twice
-            square = square + pltpu.roll(square, 2, 0)
-            square = 0.5 * (square + pltpu.roll(square, 1, 0))
-            high, middle, low = split(square)
-            parts = jnp.where(line == 0, high, jnp.where(line == 1, middle, low))
-            planes[pl.ds(to + 16, 8), :] = jnp.where(line < 3, parts, jnp.where((line == 3) | (line == 7), 0.0, 1.0))
-            weighted = jnp.where((line == 3) | (line == 7), 1.0, twice) * charge
-            high = weighted.astype(BF16).astype(F32)
-            planes[pl.ds(to + 24, 8), :] = jnp.where(upper, high, weighted - high)
-            totals[pl.ds(pl.multiple_of(step * 64, 64) + k * 8, 8), :] = zero
+            totals[pl.ds(pl.multiple_of(step * 64, 64) + k * 8, 8), :] = jnp.zeros((8, LANES), F32)
         return carry
 
-    lax.fori_loop(0, ROWS // 8, prepare, 0)
+    lax.fori_loop(0, ROWS // 8, clear, 0)
 
     sign = jnp.where(line % 4 == 3, 1.0, -1.0).astype(F32)
     live_count = live[0]
@@ -162,7 +141,7 @@
     lax.fori_loop(0, ROWS // 8, finish, 0)
 
 
-def tile_forces(tiles, live, blocks):
+def tile_forces(tiles, live, blocks, planes):
     return pl.pallas_call(
         tile_kernel,
         out_shape=jax.ShapeDtypeStruct((SLOTS, 3, CL, LANES), F32),
@@ -170,17 +149,17 @@
             pl.BlockSpec(memory_space=pltpu.SMEM),
             pl.BlockSpec(memory_space=pltpu.SMEM),
             pl.BlockSpec(memory_space=pltpu.VMEM),
+            pl.BlockSpec(memory_space=pltpu.VMEM),
         ],
         out_specs=pl.BlockSpec(memory_space=pltpu.VMEM),
         scratch_shapes=[
-            pltpu.VMEM((PLANES * ROWS, LANES), F32),
             pltpu.VMEM((ROWS * 8, LANES), F32),
             pltpu.VMEM((UNROLL // 2, 256, 256), BF16),
             pltpu.VMEM((UNROLL // 2, 256, 256), BF16),
         ],
         compiler_params=pltpu.CompilerParams(vmem_limit_bytes=40 * 2**20),
         cost_estimate=pl.CostEstimate(flops=256 * 128 * 128 * 120, bytes_accessed=2 * 2**20, transcendentals=256 * 128 * 128),
-    )(tiles, live, blocks.reshape(SLOTS * CHANNELS * CL, LANES))
+    )(tiles, live, blocks, planes)
 
 
 VMEM = pl.BlockSpec(memory_space=pltpu.VMEM)
@@ -223,43 +202,91 @@
     return barrier
 
 
+def channel(slot, c):
+    return pl.ds(pl.multiple_of(slot * (CHANNELS * CL) + c * CL, CL), CL)
+
+
+def prepare(slot, blocks, planes):
+    line = lax.broadcasted_iota(jnp.int32, (8, LANES), 0)
+    upper = line < 4
+    center = jnp.where(line < 3, CENTER, 0.0).astype(F32)
+
+    def eight_clusters(step, carry):
+        for k in range(8):
+            first = pl.multiple_of(slot * (CHANNELS * CL) + step * 8, 8) + k
+            to = pl.multiple_of(slot * (CL * PLANES) + step * (8 * PLANES), 8 * PLANES) + k * PLANES
+            loaded = blocks[pl.ds(first, 8, stride=CL), :] - center
+            twice = jnp.where(upper, loaded, pltpu.roll(loaded, 4, 0))
+            charge = jnp.broadcast_to(loaded[4:5, :], (8, LANES))
+            high, middle, low = split(twice)
+            planes[pl.ds(to, 8), :] = jnp.where(upper, high, middle)
+            planes[pl.ds(to + 8, 8), :] = jnp.where(upper, low, high)
+            square = twice * twice
+            square = square + pltpu.roll(square, 2, 0)
+            square = 0.5 * (square + pltpu.roll(square, 1, 0))
+            high, middle, low = split(square)
+            parts = jnp.where(line == 0, high, jnp.where(line == 1, middle, low))
+            planes[pl.ds(to + 16, 8), :] = jnp.where(line < 3, parts, jnp.where((line == 3) | (line == 7), 0.0, 1.0))
+            weighted = jnp.where((line == 3) | (line == 7), 1.0, twice) * charge
+            high = weighted.astype(BF16).astype(F32)
+            planes[pl.ds(to + 24, 8), :] = jnp.where(upper, high, weighted - high)
+        return carry
+
+    lax.fori_loop(0, CL // 8, eight_clusters, 0)
+
+
+def clear_unused(blocks):
+    for slot in range(SLOTS):
+        for c in range(5, CHANNELS):
+            blocks[channel(slot, c), :] = jnp.zeros((CL, LANES), F32)
+
+
 def remote(source, target, send_sems, recv_sems, way, chunk, device):
     return pltpu.make_async_remote_copy(
         source, target, send_sems.at[way, chunk], recv_sems.at[way, chunk], device_id=device, device_id_type=MESH
     )
 
 
-def spread(n, buffer, channels, send_sems, recv_sems, ready):
+def spread(n, buffer, planes, channels, send_sems, recv_sems, ready):
     sent = []
 
     def send(way, chunk, slot, there, name):
-        copy = remote(buffer.at[slot, chunk], buffer.at[there, chunk], send_sems, recv_sems, way, chunk, n[name])
+        copy = remote(buffer.at[channel(slot, chunk)], buffer.at[channel(there, chunk)], send_sems, recv_sems, way, chunk, n[name])
         copy.start()
         sent.append(copy)
 
     def arrive(way, chunk, slot):
-        remote(buffer.at[slot, chunk], buffer.at[slot, chunk], send_sems, recv_sems, way, chunk, n["core"]).wait_recv()
+        place = buffer.at[channel(slot, chunk)]
+        remote(place, place, send_sems, recv_sems, way, chunk, n["core"]).wait_recv()
 
     for c in channels:
         ready(c)
         send(1, c, n["mine"], n["other_slot"], "pair")
         send(0, c, n["mine"], n["mine"], "core")
+    prepare(n["mine"], buffer, planes)
     for c in channels:
         arrive(1, c, n["pair_slot"])
         send(2, c, n["pair_slot"], n["mine"], "cross")
         send(3, c, n["pair_slot"], n["other_slot"], "ahead")
+    prepare(n["pair_slot"], buffer, planes)
+    for c in channels:
+        arrive(0, c, n["core_slot"])
+    prepare(n["core_slot"], buffer, planes)
     for c in channels:
         arrive(2, c, n["plate_slot"])
         send(4, c, n["plate_slot"], n["plate_slot"], "core")
+    prepare(n["plate_slot"], buffer, planes)
     for c in channels:
-        arrive(0, c, n["core_slot"])
+        arrive(4, c, n["far_slot"])
+    prepare(n["far_slot"], buffer, planes)
+    for c in channels:
         arrive(3, c, n["other_slot"])
-        arrive(4, c, n["far_slot"])
+    prepare(n["other_slot"], buffer, planes)
     for copy in sent:
         copy.wait_send()
 
 
-def gather_forces(n, partial, landing, send_sems, recv_sems):
+def gather_forces(n, partial, landing, send_sems, recv_sems, meanwhile):
     sent = []
 
     def send(way, chunk, source, name):
@@ -276,6 +303,7 @@
         send(2, c, partial.at[n["other_slot"], c], "behind")
     for c in range(3):
         send(4, c, partial.at[n["core_slot"], c], "core")
+    meanwhile()
     for c in range(3):
         arrive(0, c)
         landing[5, c] = partial[n["plate_slot"], c] + landing[0, c]
@@ -294,16 +322,17 @@
     return total, sent
 
 
-def import_kernel(radii, positions, charges, types, buffer, kinds, table, load_sems, send_sems, recv_sems):
+def import_kernel(radii, positions, charges, types, buffer, planes, kinds, table, load_sems, send_sems, recv_sems):
     n = neighbours()
     mine = n["mine"]
-    loads = [pltpu.make_async_copy(positions.at[c], buffer.at[mine, c], load_sems.at[c]) for c in range(3)]
+    loads = [pltpu.make_async_copy(positions.at[c], buffer.at[channel(mine, c)], load_sems.at[c]) for c in range(3)]
     loads.append(pltpu.make_async_copy(types, kinds, load_sems.at[3]))
-    loads.append(pltpu.make_async_copy(charges, buffer.at[mine, CHARGE], load_sems.at[4]))
+    loads.append(pltpu.make_async_copy(charges, buffer.at[channel(mine, CHARGE)], load_sems.at[4]))
     loads.append(pltpu.make_async_copy(radii, table, load_sems.at[5]))
     for load in loads:
         load.start()
     barrier = greet([n[name] for name in PARTNERS])
+    clear_unused(buffer)
     pl.semaphore_wait(barrier, len(PARTNERS))
 
     def ready(c):
@@ -313,27 +342,30 @@
             radius = jnp.zeros((CL, LANES), F32)
             for kind in range(16):
                 radius = jnp.where(kinds[...] == kind, table[kind], radius)
-            buffer[mine, RADIUS] = radius
-
-    spread(n, buffer, (0, 1, 2, CHARGE, RADIUS), send_sems, recv_sems, ready)
-
-
-def step_kernel(partial, fixed, velocities, places, moving, landing, send_sems, recv_sems, next_send, next_recv):
+            buffer[channel(mine, RADIUS), :] = radius
+
+    spread(n, buffer, planes, (0, 1, 2, CHARGE, RADIUS), send_sems, recv_sems, ready)
+
+
+def step_kernel(partial, fixed, velocities, places, planes, moving, landing, send_sems, recv_sems, next_send, next_recv):
     n = neighbours()
     mine = n["mine"]
     barrier = greet([n[name] for name in PARTNERS])
     pl.semaphore_wait(barrier, len(PARTNERS))
-    force, sent = gather_forces(n, partial, landing, send_sems, recv_sems)
+    def meanwhile():
+        for slot in range(SLOTS):
+            for c in (RADIUS, CHARGE):
+                places[channel(slot, c), :] = fixed[channel(slot, c), :]
+        clear_unused(places)
+
+    force, sent = gather_forces(n, partial, landing, send_sems, recv_sems, meanwhile)
 
     def ready(c):
         speed = velocities[c] + time_step * force(c)
         moving[c] = speed
-        places[mine, c] = fixed[mine, c] + time_step * speed
-
-    for slot in range(SLOTS):
-        for c in (RADIUS, CHARGE):
-            places[slot, c] = fixed[slot, c]
-    spread(n, places, range(3), next_send, next_recv, ready)
+        places[channel(mine, c), :] = fixed[channel(mine, c), :] + time_step * speed
+
+    spread(n, places, planes, range(3), next_send, next_recv, ready)
     for copy in sent:
         copy.wait_send()
 
@@ -356,19 +388,21 @@
     select = (lax.broadcasted_iota(jnp.int32, (ARRIVING, CL), 0).astype(F32) == slot).astype(BF16)
 
     pl.semaphore_wait(barrier, 2 + TOWERS - 1)
-    force, sent = gather_forces(n, partial, landing, send_sems, recv_sems)
-    carried = []
-    speeds = []
+    def keep(k, value):
+        parts = split(value)
+        slots[:, k, :] = sum(jnp.dot(select, part.astype(BF16), preferred_element_type=F32) for part in reversed(parts))
+
+    def meanwhile():
+        keep(6, places[channel(mine, CHARGE), :])
+        keep(7, places[channel(mine, RADIUS), :])
+
+    force, sent = gather_forces(n, partial, landing, send_sems, recv_sems, meanwhile)
     for k in range(3):
         total = force(k)
         forces_out[k] = total
         speed = moving[k] + time_step * total
-        speeds.append(speed)
-        carried.append(places[mine, k] + time_step * speed)
-    carried = carried + speeds + [places[mine, CHARGE], places[mine, RADIUS]]
-    for k, value in enumerate(carried):
-        parts = split(value)
-        slots[:, k, :] = sum(jnp.dot(select, part.astype(BF16), preferred_element_type=F32) for part in reversed(parts))
+        keep(3 + k, speed)
+        keep(k, places[channel(mine, k), :] + time_step * speed)
 
     def send(tower):
         return pltpu.make_async_remote_copy(
@@ -417,25 +451,27 @@
     held = functools.partial(pltpu.with_memory_space_constraint, memory_space=pltpu.HBM)
     shape = functools.partial(jax.ShapeDtypeStruct, dtype=F32)
     pairs = tiles.T
+    blocks = shape((SLOTS * CHANNELS * CL, LANES))
+    operands = shape((ROWS * PLANES, LANES))
     landing = pltpu.VMEM((7, 3, CL, LANES), F32)
-    fixed = pl.pallas_call(
+    fixed, planes = pl.pallas_call(
         import_kernel,
-        out_shape=shape((SLOTS, CHANNELS, CL, LANES)),
+        out_shape=(blocks, operands),
         in_specs=[HBM] * 4,
-        out_specs=VMEM,
+        out_specs=(VMEM, VMEM),
         scratch_shapes=[pltpu.VMEM((CL, LANES), jnp.int32), pltpu.SMEM((16,), F32), dma(6), dma(5, 5), dma(5, 5)],
         compiler_params=params(0),
     )(*(held(v) for v in (type_radius, jnp.swapaxes(positions, 0, 1), charges, atom_types)))
-    partial = tile_forces(pairs, tile_live, fixed)
-    places, moving = pl.pallas_call(
+    partial = tile_forces(pairs, tile_live, fixed, planes)
+    places, planes, moving = pl.pallas_call(
         step_kernel,
-        out_shape=(shape((SLOTS, CHANNELS, CL, LANES)), shape((3, CL, LANES))),
+        out_shape=(blocks, operands, shape((3, CL, LANES))),
         in_specs=[VMEM] * 3,
-        out_specs=(VMEM, VMEM),
+        out_specs=(VMEM, VMEM, VMEM),
         scratch_shapes=[landing, dma(5, 3), dma(5, 3), dma(5, 3), dma(5, 3)],
         compiler_params=params(1),
     )(partial, fixed, jnp.swapaxes(velocities, 0, 1))
-    partial = tile_forces(pairs, tile_live, places)
+    partial = tile_forces(pairs, tile_live, places, planes)
     forces, arrived = pl.pallas_call(
         last_kernel,
         out_shape=(shape((3, CL, LANES)), shape((ARRIVING, 8, LANES))),

time: 86.5 us -> 84.6 us (0.978)
  Pallas kernels: 83.4 us -> 80.9 us
    pallas_call x2, Pallas kernels: 27.9 us -> 22.1 us  [tile_forces(): pl.pallas_call(tile_kernel, out_shape=jax.ShapeDtypeStruct((SLOTS, 3, CL,...]
    pallas_call x1, Pallas kernels: 19.9 us -> 21.6 us  [local(): pl.pallas_call(last_kernel, out_shape=(shape((3, CL, LANES)), shape((ARRI...]
    pallas_call x2, Pallas kernels: 35.5 us -> 37.1 us  [the longest x1 19.1 us: local(): pl.pallas_call(step_kernel, out_shape=(blocks, operands, shape((3, CL, LA...]
where the time goes in v4:
time: 84.6 us; the launch traced here: 84.4 us
  Pallas kernels  80.9 us (96%)
  local copies, waits for them, and re-layouts  2.12 us (3%)
  between operations  1.39 us (2%)
    pallas_call x2, Pallas kernels, tile_forces(): pl.pallas_call(tile_kernel, out_shape=jax.ShapeDtypeStruct((SLOTS, 3, CL,...  22.1 us
    pallas_call x1, Pallas kernels, local(): pl.pallas_call(last_kernel, out_shape=(shape((3, CL, LANES)), shape((ARRI...  21.6 us
    pallas_call x1, Pallas kernels, local(): pl.pallas_call(step_kernel, out_shape=(blocks, operands, shape((3, CL, LA...  19.1 us
    pallas_call x1, Pallas kernels, local(): pl.pallas_call(import_kernel, out_shape=(blocks, operands), in_specs=[HBM...  18.1 us
    unnamed x8, local copies, waits for them, and re-layouts  2.12 us

profile of v4, /device:TPU:0, one launch (start us, length us, event | category | flops | bytes accessed | tf_op | source)
XLA Modules:
  0.0 84.4 jit_solution(17220343159798463972)
XLA Ops:
  0.6 0.0 copy-start
  1.3 18.1 %shard_map.95 = (f32[3072,128]{1,0:T(8,128)S(1)}, f32[12288,128]{1,0:T(8,128)S(1)}) custom-call(f32[16]{0:T(128)} %radii.1, f32[3,64,128]{2,1,0:T(8,128)} %bitcast.10, f32[64,128]{1,0:T(8,128)} %charges.1, s32[64,128]{1,0:T(8,128)} %types.1), custom_call_target="tpu_custom_call" | custom-call | tf_op jit(solution)/shard_map/pallas_call | solution.py:457
  19.4 0.0 copy-start.1
  19.4 0.7 copy-done.1
  20.1 11.0 %shard_map.96.partial = f32[6,3,64,128]{3,2,1,0:T(8,128)S(1)} custom-call(s32[2,256]{1,0:T(2,128)S(1)} %bitcast.7, s32[1]{0:T(128)S(6)} %copy.12.live, f32[3072,128]{1,0:T(8,128)S(1)} %get-tuple-element.9.blocks.fixed, f32[12288,128]{1,0:T(8,128)S(1)} %get-tuple-element.10.planes), custom_call_target="tpu_custom_call" | custom-call | flops 503316480 | bytes 2097152 | tf_op jit(solution)/shard_map/pallas_call | solution.py:145
  31.1 0.0 copy-done
  31.1 0.0 copy-start.2
  31.2 19.1 %shard_map.97 = (f32[3072,128]{1,0:T(8,128)S(1)}, f32[12288,128]{1,0:T(8,128)S(1)}, f32[3,64,128]{2,1,0:T(8,128)S(1)}) custom-call(f32[6,3,64,128]{3,2,1,0:T(8,128)S(1)} %shard_map.96.partial, f32[3072,128]{1,0:T(8,128)S(1)} %get-tuple-element.9.blocks.fixed, f32[3,64,128]{2,1,0:T(8,128)S(1)} %bitcast.5), custom_call_target="tpu_custom_call" | custom-call | tf_op jit(solution)/shard_map/pallas_call | solution.py:466
  50.2 11.1 %shard_map.98.partial = f32[6,3,64,128]{3,2,1,0:T(8,128)S(1)} custom-call(s32[2,256]{1,0:T(2,128)S(1)} %bitcast.8, s32[1]{0:T(128)S(6)} %copy.12.live, f32[3072,128]{1,0:T(8,128)S(1)} %get-tuple-element.11.blocks.places, f32[12288,128]{1,0:T(8,128)S(1)} %get-tuple-element.12.planes), custom_call_target="tpu_custom_call" | custom-call | flops 503316480 | bytes 2097152 | tf_op jit(solution)/shard_map/pallas_call | solution.py:145
  61.3 0.0 copy-done.2
  61.3 21.6 %shard_map.99 = (f32[3,64,128]{2,1,0:T(8,128)S(1)}, f32[128,8,128]{2,1,0:T(8,128)S(1)}) custom-call(f32[6,3,64,128]{3,2,1,0:T(8,128)S(1)} %shard_map.98.partial, f32[3072,128]{1,0:T(8,128)S(1)} %get-tuple-element.11.blocks.places, f32[3,64,128]{2,1,0:T(8,128)S(1)} %get-tuple-element.13.moving, s32[1,64]{1,0:T(1,128)S(1)} %bitcast.9), custom_call_target="tpu_custom_call" | custom-call | tf_op jit(solution)/shard_map/pallas_call | solution.py:475
  83.0 0.6 copy.13
  83.6 0.8 copy.14
Async XLA Ops:
  0.6 30.5 %copy-start = (f32[64,3,128]{2,0,1:T(8,128)S(1)}, f32[64,3,128]{2,0,1:T(8,128)}, u32[]{:S(2)}) copy-start(f32[64,3,128]{2,0,1:T(8,128)} %param.9) | copy-start | bytes 294916
  19.4 0.7 copy-start.1
  31.1 30.2 %copy-start.2 = (s32[64,1]{0,1:T(1,128)S(1)}, s32[64,1]{0,1:T(1,128)}, u32[]{:S(2)}) copy-start(s32[64,1]{0,1:T(1,128)} %param.15) | copy-start | bytes 772

commit v5 on v4

--- a/solution.py
+++ b/solution.py
@@ -36,7 +36,7 @@
     return high, middle, rest - middle
 
 
-def tile_kernel(tiles, live, blocks, planes, out, totals, store_a, store_b):
+def tile_kernel(tiles, live, planes, totals, store_a, store_b):
     line = lax.broadcasted_iota(jnp.int32, (8, LANES), 0)
 
     def clear(step, carry):
@@ -112,54 +112,31 @@
         for now, later, shift in ((store_a, store_b, 1), (store_b, store_a, 2)):
             sums = []
             for pair in range(half_group):
+                sums_of(group + shift - 1, pair, now, sums)
                 powers_of(jnp.minimum(group + shift, TILES // UNROLL - 1), pair, later)
-                sums_of(group + shift - 1, pair, now, sums)
             add(sums)
         return carry
 
     lax.fori_loop(0, (live_count + 2 * UNROLL - 1) // (2 * UNROLL), two_groups, 0)
 
-    factor = coulomb * 0.5**1.5
-
-    def finish(group, carry):
-        slot, inner = group // (CL // 8), group % (CL // 8)
-        rows = pl.ds(pl.multiple_of(inner * 8, 8), 8)
-
-        def plane(c):
-            return blocks[pl.ds(pl.multiple_of(slot * (CHANNELS * CL) + c * CL + inner * 8, 8), 8), :]
-
-        def summed(channel):
-            first = pl.multiple_of(group * 64, 64) + channel
-            return totals[pl.ds(first, 8, stride=8), :] + totals[pl.ds(first + 4, 8, stride=8), :]
-
-        scale = factor * plane(4)
-        whole = summed(3)
-        for c in range(3):
-            out[slot, c, rows, :] = scale * ((plane(c) - CENTER) * whole - summed(c))
-        return carry
-
-    lax.fori_loop(0, ROWS // 8, finish, 0)
-
-
-def tile_forces(tiles, live, blocks, planes):
+
+def tile_forces(tiles, live, planes):
     return pl.pallas_call(
         tile_kernel,
-        out_shape=jax.ShapeDtypeStruct((SLOTS, 3, CL, LANES), F32),
+        out_shape=jax.ShapeDtypeStruct((ROWS * 8, LANES), F32),
         in_specs=[
             pl.BlockSpec(memory_space=pltpu.SMEM),
             pl.BlockSpec(memory_space=pltpu.SMEM),
             pl.BlockSpec(memory_space=pltpu.VMEM),
-            pl.BlockSpec(memory_space=pltpu.VMEM),
         ],
         out_specs=pl.BlockSpec(memory_space=pltpu.VMEM),
         scratch_shapes=[
-            pltpu.VMEM((ROWS * 8, LANES), F32),
             pltpu.VMEM((UNROLL // 2, 256, 256), BF16),
             pltpu.VMEM((UNROLL // 2, 256, 256), BF16),
         ],
         compiler_params=pltpu.CompilerParams(vmem_limit_bytes=40 * 2**20),
         cost_estimate=pl.CostEstimate(flops=256 * 128 * 128 * 120, bytes_accessed=2 * 2**20, transcendentals=256 * 128 * 128),
-    )(tiles, live, blocks, planes)
+    )(tiles, live, planes)
 
 
 VMEM = pl.BlockSpec(memory_space=pltpu.VMEM)
@@ -230,6 +207,28 @@
             weighted = jnp.where((line == 3) | (line == 7), 1.0, twice) * charge
             high = weighted.astype(BF16).astype(F32)
             planes[pl.ds(to + 24, 8), :] = jnp.where(upper, high, weighted - high)
+        return carry
+
+    lax.fori_loop(0, CL // 8, eight_clusters, 0)
+
+
+def finish(slot, totals, blocks, partial):
+    factor = coulomb * 0.5**1.5
+
+    def eight_clusters(step, carry):
+        rows = pl.ds(pl.multiple_of(step * 8, 8), 8)
+
+        def plane(c):
+            return blocks[pl.ds(pl.multiple_of(slot * (CHANNELS * CL) + c * CL + step * 8, 8), 8), :]
+
+        def summed(k):
+            first = pl.multiple_of(slot * (CL * 8) + step * 64, 64) + k
+            return totals[pl.ds(first, 8, stride=8), :] + totals[pl.ds(first + 4, 8, stride=8), :]
+
+        scale = factor * plane(CHARGE)
+        whole = summed(3)
+        for c in range(3):
+            partial[slot, c, rows, :] = scale * ((plane(c) - CENTER) * whole - summed(c))
         return carry
 
     lax.fori_loop(0, CL // 8, eight_clusters, 0)
@@ -286,7 +285,7 @@
         copy.wait_send()
 
 
-def gather_forces(n, partial, landing, send_sems, recv_sems, meanwhile):
+def gather_forces(n, totals, blocks, partial, landing, send_sems, recv_sems, meanwhile):
     sent = []
 
     def send(way, chunk, source, name):
@@ -298,11 +297,12 @@
         place = landing.at[way, chunk]
         remote(place, place, send_sems, recv_sems, way, chunk, n["core"]).wait_recv()
 
-    for c in range(3):
-        send(0, c, partial.at[n["far_slot"], c], "core")
-        send(2, c, partial.at[n["other_slot"], c], "behind")
-    for c in range(3):
-        send(4, c, partial.at[n["core_slot"], c], "core")
+    for way, slot, name in ((0, "far_slot", "core"), (2, "other_slot", "behind"), (4, "core_slot", "core")):
+        finish(n[slot], totals, blocks, partial)
+        for c in range(3):
+            send(way, c, partial.at[n[slot], c], name)
+    for slot in ("plate_slot", "pair_slot", "mine"):
+        finish(n[slot], totals, blocks, partial)
     meanwhile()
     for c in range(3):
         arrive(0, c)
@@ -322,13 +322,14 @@
     return total, sent
 
 
-def import_kernel(radii, positions, charges, types, buffer, planes, kinds, table, load_sems, send_sems, recv_sems):
+def import_kernel(radii, positions, charges, types, tiles, buffer, planes, pairs, kinds, table, load_sems, send_sems, recv_sems):
     n = neighbours()
     mine = n["mine"]
     loads = [pltpu.make_async_copy(positions.at[c], buffer.at[channel(mine, c)], load_sems.at[c]) for c in range(3)]
     loads.append(pltpu.make_async_copy(types, kinds, load_sems.at[3]))
     loads.append(pltpu.make_async_copy(charges, buffer.at[channel(mine, CHARGE)], load_sems.at[4]))
     loads.append(pltpu.make_async_copy(radii, table, load_sems.at[5]))
+    loads.append(pltpu.make_async_copy(tiles, pairs, load_sems.at[6]))
     for load in loads:
         load.start()
     barrier = greet([n[name] for name in PARTNERS])
@@ -343,11 +344,12 @@
             for kind in range(16):
                 radius = jnp.where(kinds[...] == kind, table[kind], radius)
             buffer[channel(mine, RADIUS), :] = radius
+            loads[6].wait()
 
     spread(n, buffer, planes, (0, 1, 2, CHARGE, RADIUS), send_sems, recv_sems, ready)
 
 
-def step_kernel(partial, fixed, velocities, places, planes, moving, landing, send_sems, recv_sems, next_send, next_recv):
+def step_kernel(totals, fixed, velocities, places, planes, moving, partial, landing, send_sems, recv_sems, next_send, next_recv):
     n = neighbours()
     mine = n["mine"]
     barrier = greet([n[name] for name in PARTNERS])
@@ -358,7 +360,7 @@
                 places[channel(slot, c), :] = fixed[channel(slot, c), :]
         clear_unused(places)
 
-    force, sent = gather_forces(n, partial, landing, send_sems, recv_sems, meanwhile)
+    force, sent = gather_forces(n, totals, fixed, partial, landing, send_sems, recv_sems, meanwhile)
 
     def ready(c):
         speed = velocities[c] + time_step * force(c)
@@ -370,8 +372,12 @@
         copy.wait_send()
 
 
+def links(k):
+    return min(k // 8, 4 - k // 8) + min(k // 2 % 4, 4 - k // 2 % 4) + k % 2
+
+
 def last_kernel(
-    partial, places, moving, destinations, forces_out, arrived, landing, slots, send_sems, recv_sems, out_sems, in_sems, own_sem
+    totals, places, moving, destinations, forces_out, arrived, partial, landing, slots, send_sems, recv_sems, out_sems, in_sems, own_sem
 ):
     z, y, x = here()
     n = neighbours()
@@ -396,7 +402,7 @@
         keep(6, places[channel(mine, CHARGE), :])
         keep(7, places[channel(mine, RADIUS), :])
 
-    force, sent = gather_forces(n, partial, landing, send_sems, recv_sems, meanwhile)
+    force, sent = gather_forces(n, totals, places, partial, landing, send_sems, recv_sems, meanwhile)
     for k in range(3):
         total = force(k)
         forces_out[k] = total
@@ -424,7 +430,7 @@
             device_id_type=MESH,
         )
 
-    for k in range(1, TOWERS):
+    for k in sorted(range(1, TOWERS), key=links, reverse=True):
         send(lax.rem(z + k, TOWERS)).start()
     own = pltpu.make_async_copy(
         slots.at[pl.ds(z * CAPACITY, CAPACITY)], arrived.at[pl.ds(z * CAPACITY, CAPACITY)], own_sem
@@ -450,34 +456,35 @@
 def local(positions, velocities, charges, atom_types, type_radius, tiles, tile_live, destinations):
     held = functools.partial(pltpu.with_memory_space_constraint, memory_space=pltpu.HBM)
     shape = functools.partial(jax.ShapeDtypeStruct, dtype=F32)
-    pairs = tiles.T
     blocks = shape((SLOTS * CHANNELS * CL, LANES))
     operands = shape((ROWS * PLANES, LANES))
+    partial = pltpu.VMEM((SLOTS, 3, CL, LANES), F32)
     landing = pltpu.VMEM((7, 3, CL, LANES), F32)
-    fixed, planes = pl.pallas_call(
+    fixed, planes, pairs = pl.pallas_call(
         import_kernel,
-        out_shape=(blocks, operands),
-        in_specs=[HBM] * 4,
-        out_specs=(VMEM, VMEM),
-        scratch_shapes=[pltpu.VMEM((CL, LANES), jnp.int32), pltpu.SMEM((16,), F32), dma(6), dma(5, 5), dma(5, 5)],
+        out_shape=(blocks, operands, jax.ShapeDtypeStruct((2, TILES), jnp.int32)),
+        in_specs=[HBM] * 5,
+        out_specs=(VMEM, VMEM, VMEM),
+        scratch_shapes=[pltpu.VMEM((CL, LANES), jnp.int32), pltpu.SMEM((16,), F32), dma(7), dma(5, 5), dma(5, 5)],
         compiler_params=params(0),
-    )(*(held(v) for v in (type_radius, jnp.swapaxes(positions, 0, 1), charges, atom_types)))
-    partial = tile_forces(pairs, tile_live, fixed, planes)
+    )(*(held(v) for v in (type_radius, jnp.swapaxes(positions, 0, 1), charges, atom_types, tiles.T)))
+    totals = tile_forces(pairs, tile_live, planes)
     places, planes, moving = pl.pallas_call(
         step_kernel,
         out_shape=(blocks, operands, shape((3, CL, LANES))),
         in_specs=[VMEM] * 3,
         out_specs=(VMEM, VMEM, VMEM),
-        scratch_shapes=[landing, dma(5, 3), dma(5, 3), dma(5, 3), dma(5, 3)],
+        scratch_shapes=[partial, landing, dma(5, 3), dma(5, 3), dma(5, 3), dma(5, 3)],
         compiler_params=params(1),
-    )(partial, fixed, jnp.swapaxes(velocities, 0, 1))
-    partial = tile_forces(pairs, tile_live, places, planes)
+    )(totals, fixed, jnp.swapaxes(velocities, 0, 1))
+    totals = tile_forces(pairs, tile_live, planes)
     forces, arrived = pl.pallas_call(
         last_kernel,
         out_shape=(shape((3, CL, LANES)), shape((ARRIVING, 8, LANES))),
         in_specs=[VMEM] * 4,
         out_specs=(VMEM, VMEM),
         scratch_shapes=[
+            partial,
             landing,
             pltpu.VMEM((ARRIVING, 8, LANES), F32),
             dma(5, 3),
@@ -487,7 +494,7 @@
             pltpu.SemaphoreType.DMA,
         ],
         compiler_params=params(2),
-    )(partial, places, moving, destinations.T)
+    )(totals, places, moving, destinations.T)
     return jnp.swapaxes(forces, 0, 1), arrived
 
 

time: 84.6 us -> 80.7 us (0.954)
  Pallas kernels: 80.9 us -> 77.7 us
    pallas_call x3, Pallas kernels: 40.2 us -> 33.7 us  [the longest x1 18.1 us: local(): pl.pallas_call(import_kernel, out_shape=(blocks, operands, jax.ShapeDtype...]
    pallas_call x1, Pallas kernels: 19.1 us -> 21.5 us  [local(): pl.pallas_call(step_kernel, out_shape=(blocks, operands, shape((3, CL, LA...]
    pallas_call x1, Pallas kernels: 21.6 us -> 22.6 us  [local(): pl.pallas_call(last_kernel, out_shape=(shape((3, CL, LANES)), shape((ARRI...]
    unnamed x8 -> x6, local copies, waits for them, and re-layouts: 2.12 us -> 1.45 us
where the time goes in v5:
time: 80.7 us; the launch traced here: 80.5 us
  Pallas kernels  77.7 us (96%)
  local copies, waits for them, and re-layouts  1.45 us (2%)
  between operations  1.35 us (2%)
    pallas_call x1, Pallas kernels, local(): pl.pallas_call(last_kernel, out_shape=(shape((3, CL, LANES)), shape((ARRI...  22.6 us
    pallas_call x1, Pallas kernels, local(): pl.pallas_call(step_kernel, out_shape=(blocks, operands, shape((3, CL, LA...  21.5 us
    pallas_call x1, Pallas kernels, local(): pl.pallas_call(import_kernel, out_shape=(blocks, operands, jax.ShapeDtype...  18.1 us
    pallas_call x2, Pallas kernels, tile_forces(): pl.pallas_call(tile_kernel, out_shape=jax.ShapeDtypeStruct((ROWS * 8, LAN...  15.6 us

profile of v5, /device:TPU:0, one launch (start us, length us, event | category | flops | bytes accessed | tf_op | source)
XLA Modules:
  0.0 80.5 jit_solution(13522891299200414217)
XLA Ops:
  1.3 18.1 %shard_map.95 = (f32[3072,128]{1,0:T(8,128)S(1)}, f32[12288,128]{1,0:T(8,128)S(1)}, s32[2,256]{1,0:T(2,128)S(1)}) custom-call(f32[16]{0:T(128)} %radii.1, f32[3,64,128]{2,1,0:T(8,128)} %bitcast.8, f32[64,128]{1,0:T(8,128)} %charges.1, s32[64,128]{1,0:T(8,128)} %types.1, s32[2,256]{1,0:T(2,128)} %bitcast.9), custom_call_target="tpu_custom_call" | custom-call | tf_op jit(solution)/shard_map/pallas_call | solution.py:463
  19.4 0.0 copy-start
  19.4 7.8 %shard_map.96.totals = f32[3072,128]{1,0:T(8,128)S(1)} custom-call(s32[2,256]{1,0:T(2,128)S(1)} %get-tuple-element.10.tiles, s32[1]{0:T(128)S(6)} %copy.12.live, f32[12288,128]{1,0:T(8,128)S(1)} %get-tuple-element.11.planes), custom_call_target="tpu_custom_call" | custom-call | flops 503316480 | bytes 2097152 | tf_op jit(solution)/shard_map/pallas_call | solution.py:124
  27.1 0.0 copy-done
  27.2 21.5 %shard_map.97 = (f32[3072,128]{1,0:T(8,128)S(1)}, f32[12288,128]{1,0:T(8,128)S(1)}, f32[3,64,128]{2,1,0:T(8,128)S(1)}) custom-call(f32[3072,128]{1,0:T(8,128)S(1)} %shard_map.96.totals, f32[3072,128]{1,0:T(8,128)S(1)} %get-tuple-element.12.fixed, f32[3,64,128]{2,1,0:T(8,128)S(1)} %bitcast.5), custom_call_target="tpu_custom_call" | custom-call | tf_op jit(solution)/shard_map/pallas_call | solution.py:472
  48.6 0.0 copy-start.1
  48.6 7.8 %shard_map.98.totals = f32[3072,128]{1,0:T(8,128)S(1)} custom-call(s32[2,256]{1,0:T(2,128)S(1)} %get-tuple-element.10.tiles, s32[1]{0:T(128)S(6)} %copy.12.live, f32[12288,128]{1,0:T(8,128)S(1)} %get-tuple-element.13.planes), custom_call_target="tpu_custom_call" | custom-call | flops 503316480 | bytes 2097152 | tf_op jit(solution)/shard_map/pallas_call | solution.py:124
  56.5 0.0 copy-done.1
  56.5 22.6 %shard_map.99 = (f32[3,64,128]{2,1,0:T(8,128)S(1)}, f32[128,8,128]{2,1,0:T(8,128)S(1)}) custom-call(f32[3072,128]{1,0:T(8,128)S(1)} %shard_map.98.totals, f32[3072,128]{1,0:T(8,128)S(1)} %get-tuple-element.14.places, f32[3,64,128]{2,1,0:T(8,128)S(1)} %get-tuple-element.15.moving, s32[1,64]{1,0:T(1,128)S(1)} %bitcast.7), custom_call_target="tpu_custom_call" | custom-call | tf_op jit(solution)/shard_map/pallas_call | solution.py:481
  79.1 0.6 copy.13
  79.7 0.8 copy.14
Async XLA Ops:
  19.4 7.8 %copy-start = (f32[64,3,128]{2,0,1:T(8,128)S(1)}, f32[64,3,128]{2,0,1:T(8,128)}, u32[]{:S(2)}) copy-start(f32[64,3,128]{2,0,1:T(8,128)} %param.9) | copy-start | bytes 294916
  48.6 7.9 %copy-start.1 = (s32[64,1]{0,1:T(1,128)S(1)}, s32[64,1]{0,1:T(1,128)}, u32[]{:S(2)}) copy-start(s32[64,1]{0,1:T(1,128)} %param.15) | copy-start | bytes 772

commit v6 on v5

--- a/solution.py
+++ b/solution.py
@@ -36,7 +36,9 @@
     return high, middle, rest - middle
 
 
-def tile_kernel(tiles, live, planes, totals, store_a, store_b):
+def tile_kernel(listed, live, planes, totals, tiles, list_sem, store_a, store_b):
+    listing = pltpu.make_async_copy(listed, tiles, list_sem)
+    listing.start()
     line = lax.broadcasted_iota(jnp.int32, (8, LANES), 0)
 
     def clear(step, carry):
@@ -45,6 +47,7 @@
         return carry
 
     lax.fori_loop(0, ROWS // 8, clear, 0)
+    listing.wait()
 
     sign = jnp.where(line % 4 == 3, 1.0, -1.0).astype(F32)
     live_count = live[0]
@@ -125,12 +128,14 @@
         tile_kernel,
         out_shape=jax.ShapeDtypeStruct((ROWS * 8, LANES), F32),
         in_specs=[
-            pl.BlockSpec(memory_space=pltpu.SMEM),
+            pl.BlockSpec(memory_space=pltpu.VMEM),
             pl.BlockSpec(memory_space=pltpu.SMEM),
             pl.BlockSpec(memory_space=pltpu.VMEM),
         ],
         out_specs=pl.BlockSpec(memory_space=pltpu.VMEM),
         scratch_shapes=[
+            pltpu.SMEM((2, TILES), jnp.int32),
+            pltpu.SemaphoreType.DMA,
             pltpu.VMEM((UNROLL // 2, 256, 256), BF16),
             pltpu.VMEM((UNROLL // 2, 256, 256), BF16),
         ],

time: 80.7 us -> 81.6 us (1.011)
  Pallas kernels: 77.7 us -> 78.6 us
    pallas_call x2, Pallas kernels: 15.6 us -> 17.2 us  [tile_forces(): pl.pallas_call(tile_kernel, out_shape=jax.ShapeDtypeStruct((ROWS * 8, LAN...]
where the time goes in v6:
time: 81.6 us; the launch traced here: 81.4 us
  Pallas kernels  78.6 us (96%)
  local copies, waits for them, and re-layouts  1.45 us (2%)
  between operations  1.35 us (2%)
    pallas_call x1, Pallas kernels, local(): pl.pallas_call(last_kernel, out_shape=(shape((3, CL, LANES)), shape((ARRI...  22.1 us
    pallas_call x1, Pallas kernels, local(): pl.pallas_call(step_kernel, out_shape=(blocks, operands, shape((3, CL, LA...  21.2 us
    pallas_call x1, Pallas kernels, local(): pl.pallas_call(import_kernel, out_shape=(blocks, operands, jax.ShapeDtype...  18.1 us
    pallas_call x2, Pallas kernels, tile_forces(): pl.pallas_call(tile_kernel, out_shape=jax.ShapeDtypeStruct((ROWS * 8, LAN...  17.2 us

profile of v6, /device:TPU:0, one launch (start us, length us, event | category | flops | bytes accessed | tf_op | source)
XLA Modules:
  0.0 81.4 jit_solution(6918300319015277266)
XLA Ops:
  1.3 18.1 %shard_map.95 = (f32[3072,128]{1,0:T(8,128)S(1)}, f32[12288,128]{1,0:T(8,128)S(1)}, s32[2,256]{1,0:T(2,128)S(1)}) custom-call(f32[16]{0:T(128)} %radii.1, f32[3,64,128]{2,1,0:T(8,128)} %bitcast.8, f32[64,128]{1,0:T(8,128)} %charges.1, s32[64,128]{1,0:T(8,128)} %types.1, s32[2,256]{1,0:T(2,128)} %bitcast.9), custom_call_target="tpu_custom_call" | custom-call | tf_op jit(solution)/shard_map/pallas_call | solution.py:468
  19.4 0.0 copy-start
  19.4 8.6 %shard_map.96.totals = f32[3072,128]{1,0:T(8,128)S(1)} custom-call(s32[2,256]{1,0:T(2,128)S(1)} %get-tuple-element.10.listed, s32[1]{0:T(128)S(6)} %copy.12.live, f32[12288,128]{1,0:T(8,128)S(1)} %get-tuple-element.11.planes), custom_call_target="tpu_custom_call" | custom-call | flops 503316480 | bytes 2097152 | tf_op jit(solution)/shard_map/pallas_call | solution.py:127
  28.0 0.0 copy-done
  28.0 21.2 %shard_map.97 = (f32[3072,128]{1,0:T(8,128)S(1)}, f32[12288,128]{1,0:T(8,128)S(1)}, f32[3,64,128]{2,1,0:T(8,128)S(1)}) custom-call(f32[3072,128]{1,0:T(8,128)S(1)} %shard_map.96.totals, f32[3072,128]{1,0:T(8,128)S(1)} %get-tuple-element.12.fixed, f32[3,64,128]{2,1,0:T(8,128)S(1)} %bitcast.5), custom_call_target="tpu_custom_call" | custom-call | tf_op jit(solution)/shard_map/pallas_call | solution.py:477
  49.2 0.0 copy-start.1
  49.2 8.7 %shard_map.98.totals = f32[3072,128]{1,0:T(8,128)S(1)} custom-call(s32[2,256]{1,0:T(2,128)S(1)} %get-tuple-element.10.listed, s32[1]{0:T(128)S(6)} %copy.12.live, f32[12288,128]{1,0:T(8,128)S(1)} %get-tuple-element.13.planes), custom_call_target="tpu_custom_call" | custom-call | flops 503316480 | bytes 2097152 | tf_op jit(solution)/shard_map/pallas_call | solution.py:127
  57.8 0.0 copy-done.1
  57.9 22.1 %shard_map.99 = (f32[3,64,128]{2,1,0:T(8,128)S(1)}, f32[128,8,128]{2,1,0:T(8,128)S(1)}) custom-call(f32[3072,128]{1,0:T(8,128)S(1)} %shard_map.98.totals, f32[3072,128]{1,0:T(8,128)S(1)} %get-tuple-element.14.places, f32[3,64,128]{2,1,0:T(8,128)S(1)} %get-tuple-element.15.moving, s32[1,64]{1,0:T(1,128)S(1)} %bitcast.7), custom_call_target="tpu_custom_call" | custom-call | tf_op jit(solution)/shard_map/pallas_call | solution.py:486
  80.0 0.6 copy.13
  80.7 0.8 copy.14
Async XLA Ops:
  19.4 8.6 %copy-start = (f32[64,3,128]{2,0,1:T(8,128)S(1)}, f32[64,3,128]{2,0,1:T(8,128)}, u32[]{:S(2)}) copy-start(f32[64,3,128]{2,0,1:T(8,128)} %param.9) | copy-start | bytes 294916
  49.2 8.7 %copy-start.1 = (s32[64,1]{0,1:T(1,128)S(1)}, s32[64,1]{0,1:T(1,128)}, u32[]{:S(2)}) copy-start(s32[64,1]{0,1:T(1,128)} %param.15) | copy-start | bytes 772

commit v7 on v6

--- a/solution.py
+++ b/solution.py
@@ -22,7 +22,7 @@
 TILES = 256
 TOWERS = 32
 ARRIVING = TOWERS * CAPACITY
-UNROLL = 16
+UNROLL = 32
 CENTER = 2.0
 PLANES = 32
 CHANNELS = 8

time: 81.6 us -> 80.5 us (0.987)
  Pallas kernels: 78.6 us -> 77.5 us
    pallas_call x1, Pallas kernels: 22.1 us -> 20.7 us  [local(): pl.pallas_call(last_kernel, out_shape=(shape((3, CL, LANES)), shape((ARRI...]
    pallas_call x2, Pallas kernels: 17.2 us -> 18.7 us  [tile_forces(): pl.pallas_call(tile_kernel, out_shape=jax.ShapeDtypeStruct((ROWS * 8, LAN...]
    pallas_call x1, Pallas kernels: 21.2 us -> 20.1 us  [local(): pl.pallas_call(step_kernel, out_shape=(blocks, operands, shape((3, CL, LA...]
where the time goes in v7:
time: 80.5 us; the launch traced here: 80.3 us
  Pallas kernels  77.5 us (96%)
  local copies, waits for them, and re-layouts  1.45 us (2%)
  between operations  1.35 us (2%)
    pallas_call x1, Pallas kernels, local(): pl.pallas_call(last_kernel, out_shape=(shape((3, CL, LANES)), shape((ARRI...  20.7 us
    pallas_call x1, Pallas kernels, local(): pl.pallas_call(step_kernel, out_shape=(blocks, operands, shape((3, CL, LA...  20.1 us
    pallas_call x2, Pallas kernels, tile_forces(): pl.pallas_call(tile_kernel, out_shape=jax.ShapeDtypeStruct((ROWS * 8, LAN...  18.7 us
    pallas_call x1, Pallas kernels, local(): pl.pallas_call(import_kernel, out_shape=(blocks, operands, jax.ShapeDtype...  18.1 us

profile of v7, /device:TPU:0, one launch (start us, length us, event | category | flops | bytes accessed | tf_op | source)
XLA Modules:
  0.0 80.3 jit_solution(2767976253352069661)
XLA Ops:
  1.3 18.1 %shard_map.95 = (f32[3072,128]{1,0:T(8,128)S(1)}, f32[12288,128]{1,0:T(8,128)S(1)}, s32[2,256]{1,0:T(2,128)S(1)}) custom-call(f32[16]{0:T(128)} %radii.1, f32[3,64,128]{2,1,0:T(8,128)} %bitcast.8, f32[64,128]{1,0:T(8,128)} %charges.1, s32[64,128]{1,0:T(8,128)} %types.1, s32[2,256]{1,0:T(2,128)} %bitcast.9), custom_call_target="tpu_custom_call" | custom-call | tf_op jit(solution)/shard_map/pallas_call | solution.py:468
  19.4 0.0 copy-start
  19.4 9.3 %shard_map.96.totals = f32[3072,128]{1,0:T(8,128)S(1)} custom-call(s32[2,256]{1,0:T(2,128)S(1)} %get-tuple-element.10.listed, s32[1]{0:T(128)S(6)} %copy.12.live, f32[12288,128]{1,0:T(8,128)S(1)} %get-tuple-element.11.planes), custom_call_target="tpu_custom_call" | custom-call | flops 503316480 | bytes 2097152 | tf_op jit(solution)/shard_map/pallas_call | solution.py:127
  28.7 0.0 copy-done
  28.7 20.1 %shard_map.97 = (f32[3072,128]{1,0:T(8,128)S(1)}, f32[12288,128]{1,0:T(8,128)S(1)}, f32[3,64,128]{2,1,0:T(8,128)S(1)}) custom-call(f32[3072,128]{1,0:T(8,128)S(1)} %shard_map.96.totals, f32[3072,128]{1,0:T(8,128)S(1)} %get-tuple-element.12.fixed, f32[3,64,128]{2,1,0:T(8,128)S(1)} %bitcast.5), custom_call_target="tpu_custom_call" | custom-call | tf_op jit(solution)/shard_map/pallas_call | solution.py:477
  48.8 0.0 copy-start.1
  48.8 9.4 %shard_map.98.totals = f32[3072,128]{1,0:T(8,128)S(1)} custom-call(s32[2,256]{1,0:T(2,128)S(1)} %get-tuple-element.10.listed, s32[1]{0:T(128)S(6)} %copy.12.live, f32[12288,128]{1,0:T(8,128)S(1)} %get-tuple-element.13.planes), custom_call_target="tpu_custom_call" | custom-call | flops 503316480 | bytes 2097152 | tf_op jit(solution)/shard_map/pallas_call | solution.py:127
  58.2 0.0 copy-done.1
  58.2 20.7 %shard_map.99 = (f32[3,64,128]{2,1,0:T(8,128)S(1)}, f32[128,8,128]{2,1,0:T(8,128)S(1)}) custom-call(f32[3072,128]{1,0:T(8,128)S(1)} %shard_map.98.totals, f32[3072,128]{1,0:T(8,128)S(1)} %get-tuple-element.14.places, f32[3,64,128]{2,1,0:T(8,128)S(1)} %get-tuple-element.15.moving, s32[1,64]{1,0:T(1,128)S(1)} %bitcast.7), custom_call_target="tpu_custom_call" | custom-call | tf_op jit(solution)/shard_map/pallas_call | solution.py:486
  78.9 0.6 copy.13
  79.6 0.8 copy.14
Async XLA Ops:
  19.4 9.3 %copy-start = (f32[64,3,128]{2,0,1:T(8,128)S(1)}, f32[64,3,128]{2,0,1:T(8,128)}, u32[]{:S(2)}) copy-start(f32[64,3,128]{2,0,1:T(8,128)} %param.9) | copy-start | bytes 294916
  48.8 9.4 %copy-start.1 = (s32[64,1]{0,1:T(1,128)S(1)}, s32[64,1]{0,1:T(1,128)}, u32[]{:S(2)}) copy-start(s32[64,1]{0,1:T(1,128)} %param.15) | copy-start | bytes 772

commit v8 on v7

--- a/solution.py
+++ b/solution.py
@@ -302,7 +302,7 @@
         place = landing.at[way, chunk]
         remote(place, place, send_sems, recv_sems, way, chunk, n["core"]).wait_recv()
 
-    for way, slot, name in ((0, "far_slot", "core"), (2, "other_slot", "behind"), (4, "core_slot", "core")):
+    for way, slot, name in ((2, "other_slot", "behind"), (0, "far_slot", "core"), (4, "core_slot", "core")):
         finish(n[slot], totals, blocks, partial)
         for c in range(3):
             send(way, c, partial.at[n[slot], c], name)
@@ -397,11 +397,13 @@
     rank = jnp.sum(jnp.where((column == row) & (r < c), 1.0, 0.0), axis=0, keepdims=True)
     slot = row[0:1] * CAPACITY + rank
     select = (lax.broadcasted_iota(jnp.int32, (ARRIVING, CL), 0).astype(F32) == slot).astype(BF16)
+    select = jnp.concatenate([select] * 3, axis=1)
 
     pl.semaphore_wait(barrier, 2 + TOWERS - 1)
     def keep(k, value):
         parts = split(value)
-        slots[:, k, :] = sum(jnp.dot(select, part.astype(BF16), preferred_element_type=F32) for part in reversed(parts))
+        stacked = jnp.concatenate([part.astype(BF16) for part in reversed(parts)], axis=0)
+        slots[:, k, :] = jnp.dot(select, stacked, preferred_element_type=F32)
 
     def meanwhile():
         keep(6, places[channel(mine, CHARGE), :])

time: 80.5 us -> 80.3 us (level)
    pallas_call x2, Pallas kernels: 18.7 us -> 10.7 us  [tile_forces(): pl.pallas_call(tile_kernel, out_shape=jax.ShapeDtypeStruct((ROWS * 8, LAN...]
    pallas_call x1, Pallas kernels: 20.7 us -> 24.9 us  [local(): pl.pallas_call(last_kernel, out_shape=(shape((3, CL, LANES)), shape((ARRI...]
    pallas_call x1, Pallas kernels: 20.1 us -> 24.2 us  [local(): pl.pallas_call(step_kernel, out_shape=(blocks, operands, shape((3, CL, LA...]
where the time goes in v8:
time: 80.3 us; the launch traced here: 80.7 us
  Pallas kernels  77.9 us (97%)
  local copies, waits for them, and re-layouts  1.45 us (2%)
  between operations  1.35 us (2%)
    pallas_call x1, Pallas kernels, local(): pl.pallas_call(last_kernel, out_shape=(shape((3, CL, LANES)), shape((ARRI...  24.9 us
    pallas_call x1, Pallas kernels, local(): pl.pallas_call(step_kernel, out_shape=(blocks, operands, shape((3, CL, LA...  24.2 us
    pallas_call x1, Pallas kernels, local(): pl.pallas_call(import_kernel, out_shape=(blocks, operands, jax.ShapeDtype...  18.1 us
    pallas_call x2, Pallas kernels, tile_forces(): pl.pallas_call(tile_kernel, out_shape=jax.ShapeDtypeStruct((ROWS * 8, LAN...  10.7 us

profile of v8, /device:TPU:0, one launch (start us, length us, event | category | flops | bytes accessed | tf_op | source)
XLA Modules:
  0.0 80.7 jit_solution(2471368351819020858)
XLA Ops:
  1.3 18.1 %shard_map.95 = (f32[3072,128]{1,0:T(8,128)S(1)}, f32[12288,128]{1,0:T(8,128)S(1)}, s32[2,256]{1,0:T(2,128)S(1)}) custom-call(f32[16]{0:T(128)} %radii.1, f32[3,64,128]{2,1,0:T(8,128)} %bitcast.8, f32[64,128]{1,0:T(8,128)} %charges.1, s32[64,128]{1,0:T(8,128)} %types.1, s32[2,256]{1,0:T(2,128)} %bitcast.9), custom_call_target="tpu_custom_call" | custom-call | tf_op jit(solution)/shard_map/pallas_call | solution.py:470
  19.4 0.0 copy-start
  19.4 5.3 %shard_map.96.totals = f32[3072,128]{1,0:T(8,128)S(1)} custom-call(s32[2,256]{1,0:T(2,128)S(1)} %get-tuple-element.10.listed, s32[1]{0:T(128)S(6)} %copy.12.live, f32[12288,128]{1,0:T(8,128)S(1)} %get-tuple-element.11.planes), custom_call_target="tpu_custom_call" | custom-call | flops 503316480 | bytes 2097152 | tf_op jit(solution)/shard_map/pallas_call | solution.py:127
  24.7 0.0 copy-done
  24.7 24.2 %shard_map.97 = (f32[3072,128]{1,0:T(8,128)S(1)}, f32[12288,128]{1,0:T(8,128)S(1)}, f32[3,64,128]{2,1,0:T(8,128)S(1)}) custom-call(f32[3072,128]{1,0:T(8,128)S(1)} %shard_map.96.totals, f32[3072,128]{1,0:T(8,128)S(1)} %get-tuple-element.12.fixed, f32[3,64,128]{2,1,0:T(8,128)S(1)} %bitcast.5), custom_call_target="tpu_custom_call" | custom-call | tf_op jit(solution)/shard_map/pallas_call | solution.py:479
  48.9 0.0 copy-start.1
  48.9 5.4 %shard_map.98.totals = f32[3072,128]{1,0:T(8,128)S(1)} custom-call(s32[2,256]{1,0:T(2,128)S(1)} %get-tuple-element.10.listed, s32[1]{0:T(128)S(6)} %copy.12.live, f32[12288,128]{1,0:T(8,128)S(1)} %get-tuple-element.13.planes), custom_call_target="tpu_custom_call" | custom-call | flops 503316480 | bytes 2097152 | tf_op jit(solution)/shard_map/pallas_call | solution.py:127
  54.3 0.0 copy-done.1
  54.3 24.9 %shard_map.99 = (f32[3,64,128]{2,1,0:T(8,128)S(1)}, f32[128,8,128]{2,1,0:T(8,128)S(1)}) custom-call(f32[3072,128]{1,0:T(8,128)S(1)} %shard_map.98.totals, f32[3072,128]{1,0:T(8,128)S(1)} %get-tuple-element.14.places, f32[3,64,128]{2,1,0:T(8,128)S(1)} %get-tuple-element.15.moving, s32[1,64]{1,0:T(1,128)S(1)} %bitcast.7), custom_call_target="tpu_custom_call" | custom-call | tf_op jit(solution)/shard_map/pallas_call | solution.py:488
  79.2 0.6 copy.13
  79.9 0.8 copy.14
Async XLA Ops:
  19.4 5.3 %copy-start = (f32[64,3,128]{2,0,1:T(8,128)S(1)}, f32[64,3,128]{2,0,1:T(8,128)}, u32[]{:S(2)}) copy-start(f32[64,3,128]{2,0,1:T(8,128)} %param.9) | copy-start | bytes 294916
  48.9 5.4 %copy-start.1 = (s32[64,1]{0,1:T(1,128)S(1)}, s32[64,1]{0,1:T(1,128)}, u32[]{:S(2)}) copy-start(s32[64,1]{0,1:T(1,128)} %param.15) | copy-start | bytes 772

commit v9 on v8

--- a/solution.py
+++ b/solution.py
@@ -400,22 +400,22 @@
     select = jnp.concatenate([select] * 3, axis=1)
 
     pl.semaphore_wait(barrier, 2 + TOWERS - 1)
-    def keep(k, value):
-        parts = split(value)
+    def keep(first, value, second, other):
+        parts = split(jnp.concatenate([value, other], axis=1))
         stacked = jnp.concatenate([part.astype(BF16) for part in reversed(parts)], axis=0)
-        slots[:, k, :] = jnp.dot(select, stacked, preferred_element_type=F32)
+        chosen = jnp.dot(select, stacked, preferred_element_type=F32)
+        slots[:, first, :] = chosen[:, :LANES]
+        slots[:, second, :] = chosen[:, LANES:]
 
     def meanwhile():
-        keep(6, places[channel(mine, CHARGE), :])
-        keep(7, places[channel(mine, RADIUS), :])
+        keep(6, places[channel(mine, CHARGE), :], 7, places[channel(mine, RADIUS), :])
 
     force, sent = gather_forces(n, totals, places, partial, landing, send_sems, recv_sems, meanwhile)
     for k in range(3):
         total = force(k)
         forces_out[k] = total
         speed = moving[k] + time_step * total
-        keep(3 + k, speed)
-        keep(k, places[channel(mine, k), :] + time_step * speed)
+        keep(3 + k, speed, k, places[channel(mine, k), :] + time_step * speed)
 
     def send(tower):
         return pltpu.make_async_remote_copy(

time: 80.3 us -> 80.3 us (level)
    pallas_call x2, Pallas kernels: 10.7 us -> 6.67 us  [tile_forces(): pl.pallas_call(tile_kernel, out_shape=jax.ShapeDtypeStruct((ROWS * 8, LAN...]
    pallas_call x1, Pallas kernels: 24.9 us -> 26.9 us  [local(): pl.pallas_call(last_kernel, out_shape=(shape((3, CL, LANES)), shape((ARRI...]
    pallas_call x1, Pallas kernels: 24.2 us -> 26.1 us  [local(): pl.pallas_call(step_kernel, out_shape=(blocks, operands, shape((3, CL, LA...]
where the time goes in v9:
time: 80.3 us; the launch traced here: 80.5 us
  Pallas kernels  77.7 us (97%)
  local copies, waits for them, and re-layouts  1.45 us (2%)
  between operations  1.35 us (2%)
    pallas_call x1, Pallas kernels, local(): pl.pallas_call(last_kernel, out_shape=(shape((3, CL, LANES)), shape((ARRI...  26.9 us
    pallas_call x1, Pallas kernels, local(): pl.pallas_call(step_kernel, out_shape=(blocks, operands, shape((3, CL, LA...  26.1 us
    pallas_call x1, Pallas kernels, local(): pl.pallas_call(import_kernel, out_shape=(blocks, operands, jax.ShapeDtype...  18.1 us
    pallas_call x2, Pallas kernels, tile_forces(): pl.pallas_call(tile_kernel, out_shape=jax.ShapeDtypeStruct((ROWS * 8, LAN...  6.67 us

profile of v9, /device:TPU:0, one launch (start us, length us, event | category | flops | bytes accessed | tf_op | source)
XLA Modules:
  0.0 80.5 jit_solution(9551190103516394494)
XLA Ops:
  1.3 18.1 %shard_map.95 = (f32[3072,128]{1,0:T(8,128)S(1)}, f32[12288,128]{1,0:T(8,128)S(1)}, s32[2,256]{1,0:T(2,128)S(1)}) custom-call(f32[16]{0:T(128)} %radii.1, f32[3,64,128]{2,1,0:T(8,128)} %bitcast.8, f32[64,128]{1,0:T(8,128)} %charges.1, s32[64,128]{1,0:T(8,128)} %types.1, s32[2,256]{1,0:T(2,128)} %bitcast.9), custom_call_target="tpu_custom_call" | custom-call | tf_op jit(solution)/shard_map/pallas_call | solution.py:470
  19.4 0.0 copy-start
  19.4 3.3 %shard_map.96.totals = f32[3072,128]{1,0:T(8,128)S(1)} custom-call(s32[2,256]{1,0:T(2,128)S(1)} %get-tuple-element.10.listed, s32[1]{0:T(128)S(6)} %copy.12.live, f32[12288,128]{1,0:T(8,128)S(1)} %get-tuple-element.11.planes), custom_call_target="tpu_custom_call" | custom-call | flops 503316480 | bytes 2097152 | tf_op jit(solution)/shard_map/pallas_call | solution.py:127
  22.7 0.0 copy-done
  22.7 26.1 %shard_map.97 = (f32[3072,128]{1,0:T(8,128)S(1)}, f32[12288,128]{1,0:T(8,128)S(1)}, f32[3,64,128]{2,1,0:T(8,128)S(1)}) custom-call(f32[3072,128]{1,0:T(8,128)S(1)} %shard_map.96.totals, f32[3072,128]{1,0:T(8,128)S(1)} %get-tuple-element.12.fixed, f32[3,64,128]{2,1,0:T(8,128)S(1)} %bitcast.5), custom_call_target="tpu_custom_call" | custom-call | tf_op jit(solution)/shard_map/pallas_call | solution.py:479
  48.8 0.0 copy-start.1
  48.8 3.4 %shard_map.98.totals = f32[3072,128]{1,0:T(8,128)S(1)} custom-call(s32[2,256]{1,0:T(2,128)S(1)} %get-tuple-element.10.listed, s32[1]{0:T(128)S(6)} %copy.12.live, f32[12288,128]{1,0:T(8,128)S(1)} %get-tuple-element.13.planes), custom_call_target="tpu_custom_call" | custom-call | flops 503316480 | bytes 2097152 | tf_op jit(solution)/shard_map/pallas_call | solution.py:127
  52.2 0.0 copy-done.1
  52.2 26.9 %shard_map.99 = (f32[3,64,128]{2,1,0:T(8,128)S(1)}, f32[128,8,128]{2,1,0:T(8,128)S(1)}) custom-call(f32[3072,128]{1,0:T(8,128)S(1)} %shard_map.98.totals, f32[3072,128]{1,0:T(8,128)S(1)} %get-tuple-element.14.places, f32[3,64,128]{2,1,0:T(8,128)S(1)} %get-tuple-element.15.moving, s32[1,64]{1,0:T(1,128)S(1)} %bitcast.7), custom_call_target="tpu_custom_call" | custom-call | tf_op jit(solution)/shard_map/pallas_call | solution.py:488
  79.0 0.6 copy.13
  79.7 0.8 copy.14
Async XLA Ops:
  19.4 3.3 %copy-start = (f32[64,3,128]{2,0,1:T(8,128)S(1)}, f32[64,3,128]{2,0,1:T(8,128)}, u32[]{:S(2)}) copy-start(f32[64,3,128]{2,0,1:T(8,128)} %param.9) | copy-start | bytes 294916
  48.8 3.4 %copy-start.1 = (s32[64,1]{0,1:T(1,128)S(1)}, s32[64,1]{0,1:T(1,128)}, u32[]{:S(2)}) copy-start(s32[64,1]{0,1:T(1,128)} %param.15) | copy-start | bytes 772
